TPU v7x, 256 devices: a whole 4x4x8 slice. The times are simulated.
256 devices in a mesh: ctx: 16 (over y, z_lo), fsdp: 16 (over x, z_hi, core).
Axes of the slice: x: 4, y: 4, z: 8 (z_hi: 2, z_lo: 4; z = z_hi * 4 + z_lo), core: 2. Of those that a mesh axis runs over, the one named last changes fastest.
Arguments:
- features: bfloat16 [16, 2048, 12288], P('fsdp', 'ctx'), may hold values from -6 to 6
- short_weight: bfloat16 [7, 12288], P(None, 'fsdp'), may hold values from -2 to 2
- long_filter: bfloat16 [512, 256], replicated, may hold values from -1.1 to 1.1
- out_weight: bfloat16 [4096, 4096], P(None, 'fsdp'), may hold values from -0.09375 to 0.09375
Outputs:
- mixer_out: bfloat16 [16, 2048, 4096], P('fsdp', 'ctx')
All inputs are finite; a program needn't handle non-finite values.
Results may differ from a plain program's by a relative error of at most 0.0057.
Values may be sent and summed in bfloat16 or wider, within the bound.
A program may use at most 192 MiB of HBM per device.

v0:
```python
import jax
import jax.numpy as jnp
from jax import lax
from jax.sharding import PartitionSpec as P


def passed_along(array, axis, by):
    peers = lax.axis_size(axis)
    pairs = [(i, i + by) for i in range(peers) if 0 <= i + by < peers]
    return lax.ppermute(array, axis, pairs)


def toeplitz_block(filter_rows, offset, rows):
    later = lax.broadcasted_iota(jnp.int32, (rows, rows), 0)
    previous_rows = lax.broadcasted_iota(jnp.int32, (rows, rows), 1)
    position = offset * rows + later - previous_rows + rows
    return jnp.take(filter_rows, position, axis=1)


def block_term(filter_rows, block, offset):
    rows = block.shape[2]
    matrix = toeplitz_block(filter_rows, offset, rows)
    return jnp.einsum("fts,fgs->fgt", matrix, block, preferred_element_type=jnp.float32)


def shards(features, short_weight, long_filter, out_weight):
    sequence = features[0]
    rows = sequence.shape[0]
    taps = short_weight.shape[0]
    filters = long_filter.shape[1]
    reach = long_filter.shape[0] // rows
    prior = passed_along(sequence[rows - (taps - 1) :], "ctx", 1)
    tap_full = lax.all_gather(short_weight, "fsdp", axis=1, tiled=True).astype(jnp.float32)
    extended = jnp.concatenate([prior, sequence], axis=0).astype(jnp.float32)
    filtered = jnp.zeros(sequence.shape, jnp.float32)
    for tap_index in range(taps):
        begin = taps - 1 - tap_index
        filtered = filtered + tap_full[tap_index] * extended[begin : begin + rows]
    channels = filtered.shape[1] // 3
    groups = channels // filters
    query = filtered[:, :channels]
    keys = filtered[:, channels : 2 * channels]
    values = filtered[:, 2 * channels :]
    product = (keys * values).astype(jnp.bfloat16)
    product = product.reshape(rows, groups, filters).transpose(2, 1, 0)
    zero_cols = jnp.zeros((filters, rows), jnp.bfloat16)
    filter_rows = jnp.concatenate([zero_cols, long_filter.T, zero_cols], axis=1)
    accumulated = block_term(filter_rows, product, 0)
    carried = product
    for offset in range(1, reach + 1):
        carried = passed_along(carried, "ctx", 1)
        accumulated = accumulated + block_term(filter_rows, carried, offset)
    convolved = accumulated.transpose(2, 1, 0).reshape(rows, channels)
    gated = (query * convolved).astype(jnp.bfloat16)
    projected = jnp.dot(
        lax.all_gather(gated, "fsdp", axis=0, tiled=True),
        out_weight,
        preferred_element_type=jnp.float32,
    ).astype(jnp.bfloat16)
    result = lax.all_to_all(projected, "fsdp", split_axis=0, concat_axis=1, tiled=True)
    return result[None]


def solution(mesh):
    placed = (P("fsdp", "ctx", None), P(None, "fsdp"), P(), P(None, "fsdp"))
    return jax.shard_map(
        shards, mesh=mesh, in_specs=placed, out_specs=P("fsdp", "ctx", None), check_vma=False
    )
```

profile of v0, /device:TPU:16, one launch (start us, length us, event | category | flops | bytes accessed | tf_op | source)
XLA Modules:
  0.0 823.1 jit_solution(12900210200609849536)
XLA Ops:
  7.7 3.8 collective-permute-start
  11.5 4.6 copy.21
  16.2 33.1 %all_gather.6 = bf16[7,12288]{1,0:T(8,128)(2,1)S(1)} all-gather(bf16[7,768]{1,0:T(8,128)(2,1)S(1)} %copy-done.2), channel_id=1, replica_groups=mesh['ctx'=16,'fsdp'=16] {'fsdp'}, dimensions={1}, use_global_device_ids=true | all-gather | bytes 182784 | tf_op jit(solution)/shard_map/all_gather | solution.py:33
  51.6 2.8 copy.22
  54.4 4.7 maximum_convert_fusion
  59.1 24.6 %fusion.20 = f32[128,12288]{0,1:T(8,128)} fusion(f32[134,12288]{0,1:T(8,128)S(1)} %maximum_convert_fusion, f32[12288]{0:T(1024)S(1)} %bitcast.82, f32[12288]{0:T(1024)S(1)} %bitcast.81, f32[12288]{0:T(1024)S(1)} %bitcast.80, f32[12288]{0:T(1024)S(1)} %bitcast.79, f32[12288]{0:T(1024)S(1)} %bitcast.78, f32[12288]{0:T(1024)S(1)} %bitcast.77, f32[12288]{0:T(1024)S(1)} %bitcast.76), kind=kLoop, calls=%fused_computation.26 | loop fusion | flops 20447232 | bytes 50675712 | tf_op jit(solution)/shard_map/add | solution.py:38
  83.6 2.5 fusion.31
  86.8 2.8 collective-permute-start.1
  91.1 25.8 %collective-permute-done.1 = bf16[256,16,128]{2,1,0:T(8,128)(2,1)} collective-permute-done((bf16[256,16,128]{2,1,0:T(8,128)(2,1)S(1)}, bf16[256,16,128]{2,1,0:T(8,128)(2,1)}, u32[]{:S(2)}, u32[]{:S(2)}) %collective-permute-start.1) | collective-permute-done | bytes 1048608 | tf_op jit(solution)/shard_map/ppermute | solution.py:10
  116.9 1.9 collective-permute-start.2
  118.9 70.1 %gather_fusion.3 = bf16[16384,256]{1,0:T(8,128)(2,1)} fusion(bf16[256,768]{0,1:T(8,128)(2,1)S(1)} %pad_maximum_fusion, s32[16384]{0:T(1024)} %bitcast_clamp_fusion.1), kind=kCustom, calls=%fused_computation.3.clone | custom fusion | bytes 16842752 | tf_op jit(solution)/shard_map/jit(_take)/gather | solution.py:17
  189.0 12.4 %copy.27 = bf16[128,128,256]{1,0,2:T(8,128)(2,1)} copy(bf16[128,128,256]{2,1,0:T(8,128)(2,1)} %bitcast.63) | data formatting | bytes 16777216 | tf_op jit(solution)/shard_map/jit(_take)/gather | solution.py:17
  201.4 70.1 %gather_fusion.2 = bf16[16384,256]{1,0:T(8,128)(2,1)} fusion(bf16[256,768]{0,1:T(8,128)(2,1)S(1)} %pad_maximum_fusion, s32[16384]{0:T(1024)} %bitcast_clamp_fusion.2), kind=kCustom, calls=%fused_computation.2.clone | custom fusion | bytes 16842752 | tf_op jit(solution)/shard_map/jit(_take)/gather | solution.py:17
  271.5 12.5 %copy.26 = bf16[128,128,256]{1,0,2:T(8,128)(2,1)} copy(bf16[128,128,256]{2,1,0:T(8,128)(2,1)} %bitcast.64) | data formatting | bytes 16777216 | tf_op jit(solution)/shard_map/jit(_take)/gather | solution.py:17
  284.0 70.1 %gather_fusion.1 = bf16[16384,256]{1,0:T(8,128)(2,1)} fusion(bf16[256,768]{0,1:T(8,128)(2,1)S(1)} %pad_maximum_fusion, s32[16384]{0:T(1024)} %bitcast_clamp_fusion.3), kind=kCustom, calls=%fused_computation.1.clone | custom fusion | bytes 16842752 | tf_op jit(solution)/shard_map/jit(_take)/gather | solution.py:17
  354.1 12.4 %copy.25 = bf16[128,128,256]{1,0,2:T(8,128)(2,1)} copy(bf16[128,128,256]{2,1,0:T(8,128)(2,1)} %bitcast.65) | data formatting | bytes 16777216 | tf_op jit(solution)/shard_map/jit(_take)/gather | solution.py:17
  366.4 70.1 %gather_fusion = bf16[16384,256]{1,0:T(8,128)(2,1)} fusion(bf16[256,768]{0,1:T(8,128)(2,1)S(1)} %pad_maximum_fusion, s32[16384]{0:T(1024)} %bitcast_clamp_fusion.4), kind=kCustom, calls=%fused_computation.clone | custom fusion | bytes 16842752 | tf_op jit(solution)/shard_map/jit(_take)/gather | solution.py:17
  436.6 12.4 %copy.24 = bf16[128,128,256]{1,0,2:T(8,128)(2,1)} copy(bf16[128,128,256]{2,1,0:T(8,128)(2,1)} %bitcast.66) | data formatting | bytes 16777216 | tf_op jit(solution)/shard_map/jit(_take)/gather | solution.py:17
  449.0 70.1 %gather_fusion.4 = bf16[16384,256]{1,0:T(8,128)(2,1)} fusion(bf16[256,768]{0,1:T(8,128)(2,1)S(1)} %pad_maximum_fusion, s32[16384]{0:T(1024)} %bitcast_clamp_fusion), kind=kCustom, calls=%fused_computation.4.clone | custom fusion | bytes 16842752 | tf_op jit(solution)/shard_map/jit(_take)/gather | solution.py:17
  519.0 12.5 %copy.28 = bf16[128,128,256]{1,0,2:T(8,128)(2,1)} copy(bf16[128,128,256]{2,1,0:T(8,128)(2,1)} %bitcast.62) | data formatting | bytes 16777216 | tf_op jit(solution)/shard_map/jit(_take)/gather | solution.py:17
  532.0 2.1 collective-permute-start.3
  534.1 9.2 %fusion.8 = f32[256,16,128]{2,1,0:T(8,128)} fusion(bf16[128,128,256]{1,0,2:T(8,128)(2,1)} %copy.24, pred[128,128]{1,0:T(8,128)(4,1)S(1)} %fusion.45, bf16[128,16,256]{0,2,1:T(8,128)(2,1)S(1)} %bitcast.71), kind=kOutput, calls=%fused_computation.13 | convolution fusion | flops 138412032 | bytes 11550720 | tf_op jit(solution)/shard_map/fts,fgs->fgt/dot_general | solution.py:23
  543.3 9.6 %fusion.6 = f32[256,16,128]{2,1,0:T(8,128)} fusion(bf16[256,16,128]{2,1,0:T(8,128)(2,1)} %collective-permute-done.1, bf16[128,128,256]{1,0,2:T(8,128)(2,1)} %copy.25, pred[128,128]{1,0:T(8,128)(4,1)S(1)} %fusion.46), kind=kOutput, calls=%fused_computation.11 | convolution fusion | flops 138412032 | bytes 11550720 | tf_op jit(solution)/shard_map/fts,fgs->fgt/dot_general | solution.py:23
  553.0 8.4 %collective-permute-done.3 = bf16[256,16,128]{2,1,0:T(8,128)(2,1)S(1)} collective-permute-done((bf16[256,16,128]{2,1,0:T(8,128)(2,1)}, bf16[256,16,128]{2,1,0:T(8,128)(2,1)S(1)}, u32[]{:S(2)}, u32[]{:S(2)}) %collective-permute-start.3) | collective-permute-done | bytes 1048608 | tf_op jit(solution)/shard_map/ppermute | solution.py:10
  563.3 9.7 %fusion.4 = f32[256,16,128]{2,1,0:T(8,128)} fusion(bf16[256,16,128]{2,1,0:T(8,128)(2,1)} %collective-permute-done.2, bf16[128,128,256]{1,0,2:T(8,128)(2,1)} %copy.26, pred[128,128]{1,0:T(8,128)(4,1)S(1)} %fusion.47), kind=kOutput, calls=%fused_computation.9 | convolution fusion | flops 138412032 | bytes 11550720 | tf_op jit(solution)/shard_map/fts,fgs->fgt/dot_general | solution.py:23
  573.0 5.8 fusion.2
  578.8 11.0 %collective-permute-done.4 = bf16[256,16,128]{2,1,0:T(8,128)(2,1)} collective-permute-done((bf16[256,16,128]{2,1,0:T(8,128)(2,1)S(1)}, bf16[256,16,128]{2,1,0:T(8,128)(2,1)}, u32[]{:S(2)}, u32[]{:S(2)}) %collective-permute-start.4) | collective-permute-done | bytes 1048608 | tf_op jit(solution)/shard_map/ppermute | solution.py:10
  589.8 8.3 %add_bitcast_fusion = f32[128,16,256]{0,1,2:T(8,128)S(1)} fusion(f32[256,16,128]{2,1,0:T(8,128)} %fusion.2, f32[256,16,128]{2,1,0:T(8,128)} %fusion.4, f32[256,16,128]{2,1,0:T(8,128)} %fusion.8, f32[256,16,128]{2,1,0:T(8,128)} %fusion.6, bf16[256,16,128]{2,1,0:T(8,128)(2,1)} %collective-permute-done.4, bf16[128,128,256]{1,0,2:T(8,128)(2,1)S(1)} %bitcast.61, ...), kind=kOutput, calls=%fused_computation.49 | convolution fusion | flops 140509184 | bytes 19939328 | tf_op jit(solution)/shard_map/fts,fgs->fgt/dot_general | solution.py:23
  598.8 2.8 fusion.32
  601.5 179.4 %all-gather.2.cloned.1.call-done = bf16[2048,4096]{0,1:T(8,128)(2,1)} async-done(((bf16[128,4096]{0,1:T(8,128)(2,1)}), bf16[2048,4096]{0,1:T(8,128)(2,1)}) %all-gather.2.cloned.1.call-update) | async-done | bytes 16777232 | tf_op jit(solution)/shard_map/all_gather | solution.py:56
  780.9 8.5 %convolution_convert_fusion = bf16[2048,256]{1,0:T(8,128)(2,1)S(1)} fusion(bf16[2048,4096]{0,1:T(8,128)(2,1)} %all-gather.2.cloned.1.call-done, bf16[4096,256]{1,0:T(8,128)(2,1)S(1)} %copy-done), kind=kOutput, calls=%fused_computation.44 | convolution fusion | flops 4295491584 | bytes 19922944 | tf_op jit(solution)/shard_map/dot_general | solution.py:55
  789.4 25.0 %all_to_all.16 = bf16[16,128,256]{2,1,0:T(8,128)(2,1)S(1)} all-to-all(bf16[16,128,256]{2,1,0:T(8,128)(2,1)S(1)} %bitcast.74), channel_id=1, replica_groups=mesh['ctx'=16,'fsdp'=16] {'fsdp'}, dimensions={0} | all-to-all | bytes 2097152 | tf_op jit(solution)/shard_map/all_to_all | solution.py:60
  (55 shorter events, 10.5 us)
Async XLA Ops:
  6.5 774.4 %copy-start = (bf16[4096,256]{1,0:T(8,128)(2,1)S(1)}, bf16[4096,256]{1,0:T(8,128)(2,1)}, u32[]{:S(2)}) copy-start(bf16[4096,256]{1,0:T(8,128)(2,1)} %param.9) | copy-start | bytes 6291460
  6.5 9.6 %copy-start.2 = (bf16[7,768]{1,0:T(8,128)(2,1)S(1)}, bf16[7,768]{1,0:T(8,128)(2,1)}, u32[]{:S(2)}) copy-start(bf16[7,768]{1,0:T(8,128)(2,1)} %param.7) | copy-start | bytes 32260
  6.5 774.4 %all-gather.2.cloned.1.call-start = ((), (), s32[]{:S(2)}) async-start(), calls=%async_computation.1 | async-start | bytes 17825792 | tf_op jit(solution)/shard_map/all_gather | solution.py:56
  7.7 43.9 %collective-permute-start = (bf16[6,12288]{1,0:T(8,128)(2,1)S(1)}, bf16[6,12288]{1,0:T(8,128)(2,1)S(1)}, u32[]{:S(2)}, u32[]{:S(2)}) collective-permute-start(bf16[6,12288]{1,0:T(8,128)(2,1)S(1)} %slice_bitcast_fusion), channel_id=1, source_target_pairs={{0,16},{16,32},{32,48},{48,64},{64,80},{80,96},{96,112},{112,128},... | collective-permute-start | bytes 442376 | tf_op jit(solution)/shard_map/ppermute | solution.py:10
  16.2 35.4 %copy-start.5 = (s32[128]{0:T(128)}, s32[128]{0:T(128)S(1)}, u32[]{:S(2)}) copy-start(s32[128]{0:T(128)S(1)} %iota_add_fusion.1) | copy-start | bytes 1540
  16.2 34.8 %copy-start.3 = (s32[128]{0:T(128)}, s32[128]{0:T(128)S(1)}, u32[]{:S(2)}) copy-start(s32[128]{0:T(128)S(1)} %iota_add_fusion.2) | copy-start | bytes 1540
  83.6 35.2 %copy-start.1 = (bf16[512,256]{1,0:T(8,128)(2,1)S(1)}, bf16[512,256]{1,0:T(8,128)(2,1)}, u32[]{:S(2)}) copy-start(bf16[512,256]{1,0:T(8,128)(2,1)} %param.8) | copy-start | bytes 786436
  86.8 30.1 %collective-permute-start.1 = (bf16[256,16,128]{2,1,0:T(8,128)(2,1)S(1)}, bf16[256,16,128]{2,1,0:T(8,128)(2,1)}, u32[]{:S(2)}, u32[]{:S(2)}) collective-permute-start(bf16[256,16,128]{2,1,0:T(8,128)(2,1)S(1)} %bitcast.73), channel_id=1, source_target_pairs={{0,16},{16,32},{32,48},{48,64},{64,80},{80,96},{96,112},{112,128},... | collective-permute-start | bytes 3145736 | tf_op jit(solution)/shard_map/ppermute | solution.py:10
  89.7 29.2 %copy-start.7 = (s32[128]{0:T(128)}, s32[128]{0:T(128)S(1)}, u32[]{:S(2)}) copy-start(s32[128]{0:T(128)S(1)} %iota_add_fusion) | copy-start | bytes 1540
  116.9 415.1 %collective-permute-start.2 = (bf16[256,16,128]{2,1,0:T(8,128)(2,1)}, bf16[256,16,128]{2,1,0:T(8,128)(2,1)}, u32[]{:S(2)}, u32[]{:S(2)}) collective-permute-start(bf16[256,16,128]{2,1,0:T(8,128)(2,1)} %collective-permute-done.1), channel_id=1, source_target_pairs={{0,16},{16,32},{32,48},{48,64},{64,80},{80,96},{96,112},{112,128},... | collective-permute-start | bytes 3145736 | tf_op jit(solution)/shard_map/ppermute | solution.py:10
  519.0 12.5 %copy-start.6 = (s32[128]{0:T(128)S(1)}, s32[128]{0:T(128)}, u32[]{:S(2)}) copy-start(s32[128]{0:T(128)} %copy-done.5) | copy-start | bytes 1540
  519.0 12.6 %copy-start.4 = (s32[128]{0:T(128)S(1)}, s32[128]{0:T(128)}, u32[]{:S(2)}) copy-start(s32[128]{0:T(128)} %copy-done.3) | copy-start | bytes 1540
  519.0 12.8 %copy-start.8 = (s32[128]{0:T(128)S(1)}, s32[128]{0:T(128)}, u32[]{:S(2)}) copy-start(s32[128]{0:T(128)} %copy-done.7) | copy-start | bytes 1540
  532.0 29.4 %collective-permute-start.3 = (bf16[256,16,128]{2,1,0:T(8,128)(2,1)}, bf16[256,16,128]{2,1,0:T(8,128)(2,1)S(1)}, u32[]{:S(2)}, u32[]{:S(2)}) collective-permute-start(bf16[256,16,128]{2,1,0:T(8,128)(2,1)} %collective-permute-done.2), channel_id=1, source_target_pairs={{0,16},{16,32},{32,48},{48,64},{64,80},{80,96},{96,112},{112,128},... | collective-permute-start | bytes 3145736 | tf_op jit(solution)/shard_map/ppermute | solution.py:10
  543.3 29.7 %slice-start.2 = ((s8[8388608]{0:T(1024)(128)(4,1)}), s8[4194304]{0:T(1024)(128)(4,1)S(1)}, s32[]{:S(2)}) async-start(s8[8388608]{0:T(1024)(128)(4,1)} %bitcast.68), calls=%async_computation.4 | async-start | bytes 8388608
  553.0 20.0 %slice-start.3 = ((s8[8388608]{0:T(1024)(128)(4,1)}), s8[4194304]{0:T(1024)(128)(4,1)S(1)}, s32[]{:S(2)}) async-start(s8[8388608]{0:T(1024)(128)(4,1)} %bitcast.68), calls=%async_computation.5 | async-start | bytes 8388608
  561.4 28.4 %collective-permute-start.4 = (bf16[256,16,128]{2,1,0:T(8,128)(2,1)S(1)}, bf16[256,16,128]{2,1,0:T(8,128)(2,1)}, u32[]{:S(2)}, u32[]{:S(2)}) collective-permute-start(bf16[256,16,128]{2,1,0:T(8,128)(2,1)S(1)} %collective-permute-done.3), channel_id=1, source_target_pairs={{0,16},{16,32},{32,48},{48,64},{64,80},{80,96},{96,112},{112,128},... | collective-permute-start | bytes 3145736 | tf_op jit(solution)/shard_map/ppermute | solution.py:10
  563.3 26.5 %slice-start = ((s8[8388608]{0:T(1024)(128)(4,1)}), s8[4194304]{0:T(1024)(128)(4,1)S(1)}, s32[]{:S(2)}) async-start(s8[8388608]{0:T(1024)(128)(4,1)} %bitcast.60), calls=%async_computation.2 | async-start | bytes 8388608
  573.0 16.8 %slice-start.1 = ((s8[8388608]{0:T(1024)(128)(4,1)}), s8[4194304]{0:T(1024)(128)(4,1)S(1)}, s32[]{:S(2)}) async-start(s8[8388608]{0:T(1024)(128)(4,1)} %bitcast.60), calls=%async_computation.3 | async-start | bytes 8388608
Sparse Core Ops, SparseCore 0:
  601.7 179.1 all-gather.1
where the time goes:
time: 840 us; the launch traced here: 823 us
  local copies, waits for them, and re-layouts  425 us (51%)
  waiting for transfers between devices  225 us (27%)
  blocking collectives  58.2 us (7%)
  matrix products  51.1 us (6%)
  other arithmetic  38.4 us (5%)
  between operations  13.6 us (2%)
  starting transfers between devices  12.6 us (2%)
    gather x10, local copies, waits for them, and re-layouts, toeplitz_block(): return jnp.take(filter_rows, position, axis=1)  413 us
    all_gather x1, waiting for transfers between devices, shards(): lax.all_gather(gated, 'fsdp', axis=0, tiled=True)  179 us
    ppermute x5, waiting for transfers between devices, passed_along(): return lax.ppermute(array, axis, pairs)  45.2 us
    dot_general x5, matrix products, block_term(): jnp.einsum('fts,fgs->fgt', matrix, block, preferred_element_type=jnp.floa...  42.6 us
    all_gather x1, blocking collectives, shards(): lax.all_gather(short_weight, 'fsdp', axis=1, tiled=True).astype(jnp.float32)  33.1 us
    all_to_all x1, blocking collectives, shards(): lax.all_to_all(projected, 'fsdp', split_axis=0, concat_axis=1, tiled=True)  25 us
    add x1, other arithmetic, shards(): filtered = filtered + tap_full[tap_index] * extended[begin:begin + rows]  24.6 us
  transfers between devices with their start and end apart: 6, of which 4 were waited for; matrix products, arithmetic and copies ran while one was open for 55% of the time, Pallas kernels for 0%

commit v1 on v0

v1 whole, which is shorter than its diff:
```python
import functools

import jax
import jax.numpy as jnp
import ml_dtypes
import numpy as np
from jax import lax
from jax.experimental import pallas as pl
from jax.experimental.pallas import tpu as pltpu
from jax.sharding import PartitionSpec as P

MESH = pl.DeviceIdType.MESH
BF16 = jnp.bfloat16
F32 = jnp.float32

ROWS = 128
CHANNELS = 4096
FILTERS = 256
TAPS = 7
SPAN = 512
HALO = 16
PEERS = 4
CHUNKS = 4
WIDTH = CHANNELS // (PEERS * CHUNKS)
CHUNK = PEERS * WIDTH
SHARDS = 16
COLS = CHANNELS // SHARDS
OUT = PEERS * COLS
TAPCOLS = 3 * CHANNELS // SHARDS


def transform_matrices():
    order = np.concatenate([np.arange(0, SPAN, 2), np.arange(1, SPAN, 2)])
    turns = (np.outer(2 * order + 1, np.arange(SPAN)) % (4 * SPAN)) * (2 * np.pi / (4 * SPAN))
    forward = np.concatenate([np.cos(turns), -np.sin(turns)], axis=0)
    high = forward.astype(ml_dtypes.bfloat16)
    low = (forward - high.astype(np.float64)).astype(ml_dtypes.bfloat16)
    scale = np.float64(1.0 / SPAN)
    back_high = (high.astype(np.float64).T * scale).astype(ml_dtypes.bfloat16)
    back_low = (low.astype(np.float64).T * scale).astype(ml_dtypes.bfloat16)
    return high, low, back_high, back_low


def dot(a, b):
    return jnp.dot(a, b, preferred_element_type=F32)


def mixer_kernel(
    feat, taps_in, filt, weight, fwd_hi_in, fwd_lo_in, inv_hi_in, inv_lo_in,
    out,
    ext, taps_all, taps, fwd_hi, fwd_lo, inv_hi, inv_lo, spec, y_hi, y_lo,
    prod, cur, prev, convs, back, gated, wts, acc, outs,
    local_sem, halo_sem, tap_send, tap_recv, zf_send, zf_recv, yf_sem, zb_send, zb_recv,
    xg_send, xg_recv, wz_send, wz_recv, wy_send, wy_recv, wm_sem, wc_send, wc_recv, o_send, o_recv,
):
    ctx, fsdp = lax.axis_index("ctx"), lax.axis_index("fsdp")
    y, zl = ctx // 4, ctx % 4
    x, zh, core = fsdp // 4, (fsdp // 2) % 2, fsdp % 2
    slot = zh * 2 + core
    far_slot = (1 - zh) * 2 + core

    def device(y_=y, zl_=zl, x_=x, zh_=zh, core_=core):
        return (y_ * 4 + zl_, (x_ * 2 + zh_) * 2 + core_)

    def remote(src, dst, send, recv, to):
        return pltpu.make_async_remote_copy(
            src_ref=src, dst_ref=dst, send_sem=send, recv_sem=recv, device_id=to, device_id_type=MESH
        )

    def ring(k, at):
        return lax.rem(at + k, PEERS)

    loads = [
        pltpu.make_async_copy(feat, ext.at[pl.ds(HALO, ROWS)], local_sem.at[0]),
        pltpu.make_async_copy(taps_in, taps_all.at[fsdp], local_sem.at[1]),
        pltpu.make_async_copy(fwd_hi_in, fwd_hi, local_sem.at[2]),
        pltpu.make_async_copy(fwd_lo_in, fwd_lo, local_sem.at[3]),
        pltpu.make_async_copy(inv_hi_in, inv_hi, local_sem.at[4]),
        pltpu.make_async_copy(inv_lo_in, inv_lo, local_sem.at[5]),
        pltpu.make_async_copy(weight, wts.at[slot], local_sem.at[6]),
    ]
    for load in loads:
        load.start()

    barrier = pltpu.get_barrier_semaphore()

    def greet(to):
        pl.semaphore_signal(barrier, inc=1, device_id=to, device_id_type=MESH)

    def greet_shard(k, carry):
        greet((ctx, lax.rem(fsdp + k, SHARDS)))
        return carry

    lax.fori_loop(1, SHARDS, greet_shard, 0)
    for k in range(1, PEERS):
        greet(device(zl_=ring(k, zl)))
        greet(device(y_=ring(k, y)))
    after, before = lax.rem(ctx + 1, 16), lax.rem(ctx + 15, 16)
    greet((after, fsdp))
    greet((before, fsdp))
    greet(device(zl_=3 - zl, zh_=1 - zh))
    greet(device(zl_=ring(2, zl), zh_=1 - zh))
    pl.semaphore_wait(barrier, SHARDS - 1 + 2 * (PEERS - 1) + 4)

    halo = remote(feat.at[pl.ds(ROWS - HALO, HALO)], ext.at[pl.ds(0, HALO)], halo_sem.at[0], halo_sem.at[1], (after, fsdp))
    halo.start()

    def tap_copy(k):
        to = lax.rem(fsdp + k, SHARDS)
        return remote(taps_in, taps_all.at[fsdp], tap_send.at[k], tap_recv.at[fsdp], (ctx, to))

    def tap_arrival(k):
        peer = lax.rem(fsdp + k, SHARDS)
        return remote(taps_in, taps_all.at[peer], tap_send.at[k], tap_recv.at[peer], (ctx, peer))

    def start_taps(k, carry):
        tap_copy(k).start()
        return carry

    lax.fori_loop(1, SHARDS, start_taps, 0)

    def quarter(ref, which):
        return ref.at[pl.ds(pl.multiple_of(which * SPAN * 2, SPAN * 2), SPAN * 2)]

    mate = device(core_=1 - core)
    mate_copy = remote(weight, wts.at[slot], wm_sem.at[0], wm_sem.at[1], mate)
    mate_copy.start()

    def far_copy(j, to_zl):
        return remote(quarter(weight, y), quarter(wts.at[slot], y), wz_send.at[j], wz_recv, device(zl_=to_zl, zh_=1 - zh))

    @pl.when(zl == 0)
    def _():
        far_copy(0, 3).start()
        far_copy(1, 2).start()

    @pl.when(zl == 3)
    def _():
        far_copy(0, 0).start()
        far_copy(1, 1).start()

    for at in (2, 3):
        loads[at].wait()
    for part in range(4):
        rows = pl.ds(part * 256, 256)
        spec[rows, :] = dot(fwd_hi[rows, :], filt[...]) + dot(fwd_lo[rows, :], filt[...])

    loads[0].wait()
    loads[1].wait()
    halo.wait_recv()

    @pl.when(ctx == 0)
    def _():
        ext[pl.ds(0, HALO), :] = jnp.zeros((HALO, 3 * CHANNELS), BF16)

    @pl.when(y == 0)
    def _():
        prev[...] = jnp.zeros(prev.shape, BF16)

    def wait_taps(k, carry):
        tap_arrival(k).wait_recv()
        return carry

    lax.fori_loop(1, SHARDS, wait_taps, 0)
    for shard in range(SHARDS):
        block = taps_all[shard].astype(F32)
        taps[:, pl.ds(shard * TAPCOLS, TAPCOLS // 2)] = block[:8]
        taps[:, pl.ds(shard * TAPCOLS + TAPCOLS // 2, TAPCOLS // 2)] = block[8:]

    def short_filter(begin):
        columns = pl.ds(pl.multiple_of(begin, 128), 128)
        rows = ext[:, columns].astype(F32)
        weights = taps[:, columns]
        total = weights[0:1] * rows[HALO:]
        for lag in range(1, TAPS):
            total = total + weights[lag : lag + 1] * pltpu.roll(rows, lag, 0)[HALO:]
        return total

    def zf_copy(i, k):
        q = ring(k, zl)
        return remote(
            prod.at[i, q], cur.at[i, pl.ds(pl.multiple_of(zl * ROWS, ROWS), ROWS)], zf_send.at[i, k], zf_recv.at[i, zl], device(zl_=q)
        )

    def zf_arrival(i, k):
        q = ring(k, zl)
        return remote(
            prod.at[i, q], cur.at[i, pl.ds(pl.multiple_of(q * ROWS, ROWS), ROWS)], zf_send.at[i, k], zf_recv.at[i, q], device(zl_=q)
        )

    def products(i, carry):
        def one(q, inner):
            for part in range(WIDTH // 128):
                begin = i * CHUNK + q * WIDTH + part * 128
                keys = short_filter(CHANNELS + begin)
                values = short_filter(2 * CHANNELS + begin)
                prod[i, q, :, part * 128 : (part + 1) * 128] = (keys * values).astype(BF16)
            return inner

        lax.fori_loop(0, PEERS, one, 0)
        for k in range(1, PEERS):
            zf_copy(i, k).start()
        cur[i, pl.ds(pl.multiple_of(zl * ROWS, ROWS), ROWS), :] = prod[i, zl]
        return carry

    lax.fori_loop(0, CHUNKS, products, 0)

    def yf_copy(i):
        return remote(cur.at[i], prev.at[i], yf_sem.at[0, i], yf_sem.at[1, i], device(y_=ring(1, y)))

    def onward(i):
        for k in range(1, PEERS):
            zf_arrival(i, k).wait_recv()

        @pl.when(y < PEERS - 1)
        def _():
            yf_copy(i).start()

    def zb_copy(i, k):
        q = ring(k, zl)
        return remote(
            convs.at[i, pl.ds(pl.multiple_of(q * ROWS, ROWS), ROWS)], back.at[i, zl], zb_send.at[i, k], zb_recv.at[i, zl], device(zl_=q)
        )

    def zb_arrival(i, k):
        q = ring(k, zl)
        return remote(
            convs.at[i, pl.ds(pl.multiple_of(q * ROWS, ROWS), ROWS)], back.at[i, q], zb_send.at[i, k], zb_recv.at[i, q], device(zl_=q)
        )

    def convolve(i):
        @pl.when(y > 0)
        def _():
            yf_copy(i).wait_recv()

        def frequencies(part, carry):
            real = pl.ds(pl.multiple_of(part * 128, 128), 128)
            imag = pl.ds(pl.multiple_of(SPAN + part * 128, 128), 128)
            new, old = cur[i], prev[i]
            cr = dot(fwd_hi[real, :], new) + dot(fwd_lo[real, :], new)
            ci = dot(fwd_hi[imag, :], new) + dot(fwd_lo[imag, :], new)
            pr = dot(fwd_hi[real, :], old) + dot(fwd_lo[real, :], old)
            pi = dot(fwd_hi[imag, :], old) + dot(fwd_lo[imag, :], old)
            sign = jnp.where(part < 2, 1.0, -1.0).astype(F32)
            a = cr - sign * pi
            b = ci + sign * pr
            hr, hi = spec[real, :], spec[imag, :]
            yr = hr * a - hi * b
            yi = hr * b + hi * a
            yr_hi, yi_hi = yr.astype(BF16), yi.astype(BF16)
            y_hi[real, :] = yr_hi
            y_hi[imag, :] = yi_hi
            y_lo[real, :] = (yr - yr_hi.astype(F32)).astype(BF16)
            y_lo[imag, :] = (yi - yi_hi.astype(F32)).astype(BF16)
            return carry

        lax.fori_loop(0, 4, frequencies, 0)

        def positions(part, carry):
            rows = pl.ds(pl.multiple_of(part * ROWS, ROWS), ROWS)
            got = dot(inv_hi[rows, :], y_hi[...]) + dot(inv_hi[rows, :], y_lo[...]) + dot(inv_lo[rows, :], y_hi[...])
            convs[i, rows, :] = got.astype(BF16)
            return carry

        lax.fori_loop(0, PEERS, positions, 0)
        for k in range(1, PEERS):
            zb_copy(i, k).start()
        back[i, zl] = convs[i, pl.ds(pl.multiple_of(zl * ROWS, ROWS), ROWS), :]

    def xg_copy(i, k):
        return remote(gated.at[i, x], gated.at[i, x], xg_send.at[i, k], xg_recv.at[i, x], device(x_=ring(k, x)))

    def xg_arrival(i, k):
        q = ring(k, x)
        return remote(gated.at[i, q], gated.at[i, q], xg_send.at[i, k], xg_recv.at[i, q], device(x_=q))

    def gate(i):
        for k in range(1, PEERS):
            zb_arrival(i, k).wait_recv()
        for q in range(PEERS):
            for part in range(WIDTH // 128):
                lanes = slice(part * 128, (part + 1) * 128)
                query = short_filter(i * CHUNK + q * WIDTH + part * 128)
                gated[i, x, :, q * WIDTH + part * 128 : q * WIDTH + (part + 1) * 128] = (query * back[i, q, :, lanes].astype(F32)).astype(BF16)
        for k in range(1, PEERS):
            xg_copy(i, k).start()

    def project(i):
        for k in range(1, PEERS):
            xg_arrival(i, k).wait_recv()
        lhs = gated[i].reshape(PEERS * ROWS, CHUNK)

        def block(j, carry):
            term = dot(lhs, wts[j, pl.ds(pl.multiple_of(i * CHUNK, CHUNK), CHUNK), :])

            @pl.when(i == 0)
            def _():
                acc[j] = term

            @pl.when(i > 0)
            def _():
                acc[j] = acc[j] + term

            return carry

        lax.fori_loop(0, PEERS, block, 0)

    def wy_copy(k):
        ref = quarter(wts.at[far_slot], y)
        return remote(ref, ref, wy_send.at[k], wy_recv.at[y], device(y_=ring(k, y)))

    def wy_arrival(k):
        ref = quarter(wts.at[far_slot], ring(k, y))
        return remote(ref, ref, wy_send.at[k], wy_recv.at[ring(k, y)], device(y_=ring(k, y)))

    def wc_copy(which):
        ref = quarter(wts.at[far_slot], which)
        return remote(ref, ref, wc_send.at[which], wc_recv.at[which], mate)

    def wc_arrival(which):
        ref = quarter(wts.at[(1 - zh) * 2 + 1 - core], which)
        return remote(ref, ref, wc_send.at[which], wc_recv.at[which], mate)

    def columns_first():
        far = quarter(wts.at[far_slot], y)
        remote(far, far, wz_send.at[0], wz_recv, device(zl_=3 - zl, zh_=1 - zh)).wait_recv()
        for k in range(1, PEERS):
            wy_copy(k).start()
        wc_copy(y).start()

    def columns_rest():
        for k in range(1, PEERS):
            wy_arrival(k).wait_recv()
            wc_copy(ring(k, y)).start()

    def columns_last():
        loads[6].wait()
        mate_copy.wait_recv()
        for which in range(PEERS):
            wc_arrival(which).wait_recv()

    for at in (4, 5):
        loads[at].wait()

    def step(t, carry):
        @pl.when(t < CHUNKS)
        def _():
            onward(t)

        @pl.when(jnp.logical_and(t >= 1, t < CHUNKS + 1))
        def _():
            convolve(t - 1)

        @pl.when(t == 1)
        def _():
            columns_first()

        @pl.when(jnp.logical_and(t >= 2, t < CHUNKS + 2))
        def _():
            gate(t - 2)

        @pl.when(t == 3)
        def _():
            columns_rest()
            columns_last()

        @pl.when(t >= 3)
        def _():
            project(t - 3)

        return carry

    lax.fori_loop(0, CHUNKS + 3, step, 0)

    mine = pl.ds(pl.multiple_of(x * OUT, OUT), OUT)

    def out_copy(k):
        q = ring(k, x)
        return remote(outs.at[q], out.at[:, mine], o_send.at[k], o_recv.at[x], device(x_=q))

    def out_arrival(k):
        q = ring(k, x)
        return remote(outs.at[q], out.at[:, pl.ds(pl.multiple_of(q * OUT, OUT), OUT)], o_send.at[k], o_recv.at[q], device(x_=q))

    def finish(q, carry):
        for j in range(PEERS):
            outs[q, :, j * COLS : (j + 1) * COLS] = acc[j, pl.ds(pl.multiple_of(q * ROWS, ROWS), ROWS), :].astype(BF16)
        return carry

    lax.fori_loop(0, PEERS, finish, 0)
    for k in range(1, PEERS):
        out_copy(k).start()
    own = pltpu.make_async_copy(outs.at[x], out.at[:, mine], local_sem.at[7])
    own.start()
    own.wait()
    for k in range(1, PEERS):
        out_arrival(k).wait_recv()

    halo.wait_send()
    mate_copy.wait_send()

    def sent_taps(k, carry):
        tap_copy(k).wait_send()
        return carry

    lax.fori_loop(1, SHARDS, sent_taps, 0)

    @pl.when(jnp.logical_or(zl == 0, zl == 3))
    def _():
        far_copy(0, 3 - zl).wait_send()
        far_copy(1, ring(2, zl)).wait_send()

    for k in range(1, PEERS):
        wy_copy(k).wait_send()
        out_copy(k).wait_send()
    for which in range(PEERS):
        wc_copy(which).wait_send()

    def sent_chunk(i, carry):
        for k in range(1, PEERS):
            zf_copy(i, k).wait_send()
            zb_copy(i, k).wait_send()
            xg_copy(i, k).wait_send()

        @pl.when(y < PEERS - 1)
        def _():
            yf_copy(i).wait_send()

        return carry

    lax.fori_loop(0, CHUNKS, sent_chunk, 0)


def shards(features, short_weight, long_filter, out_weight):
    padded = jnp.pad(short_weight, ((0, 8 - TAPS), (0, 0)))
    packed = jnp.concatenate([padded[:, : TAPCOLS // 2], padded[:, TAPCOLS // 2 :]], axis=0)
    matrices = [jnp.asarray(m) for m in transform_matrices()]
    anywhere = pl.BlockSpec(memory_space=pl.ANY)
    dma = pltpu.SemaphoreType.DMA
    result = pl.pallas_call(
        mixer_kernel,
        name="mixer",
        out_shape=jax.ShapeDtypeStruct((ROWS, CHANNELS), BF16),
        in_specs=[anywhere, anywhere, pl.BlockSpec(memory_space=pltpu.VMEM)] + [anywhere] * 5,
        out_specs=anywhere,
        scratch_shapes=[
            pltpu.VMEM((HALO + ROWS, 3 * CHANNELS), BF16),
            pltpu.VMEM((SHARDS, 16, TAPCOLS // 2), BF16),
            pltpu.VMEM((8, 3 * CHANNELS), F32),
            pltpu.VMEM((2 * SPAN, SPAN), BF16),
            pltpu.VMEM((2 * SPAN, SPAN), BF16),
            pltpu.VMEM((SPAN, 2 * SPAN), BF16),
            pltpu.VMEM((SPAN, 2 * SPAN), BF16),
            pltpu.VMEM((2 * SPAN, FILTERS), F32),
            pltpu.VMEM((2 * SPAN, WIDTH), BF16),
            pltpu.VMEM((2 * SPAN, WIDTH), BF16),
            pltpu.VMEM((CHUNKS, PEERS, ROWS, WIDTH), BF16),
            pltpu.VMEM((CHUNKS, SPAN, WIDTH), BF16),
            pltpu.VMEM((CHUNKS, SPAN, WIDTH), BF16),
            pltpu.VMEM((CHUNKS, SPAN, WIDTH), BF16),
            pltpu.VMEM((CHUNKS, PEERS, ROWS, WIDTH), BF16),
            pltpu.VMEM((CHUNKS, PEERS, ROWS, CHUNK), BF16),
            pltpu.VMEM((PEERS, CHANNELS, COLS), BF16),
            pltpu.VMEM((PEERS, PEERS * ROWS, COLS), F32),
            pltpu.VMEM((PEERS, ROWS, OUT), BF16),
            dma((8,)), dma((2,)), dma((SHARDS,)), dma((SHARDS,)),
            dma((CHUNKS, PEERS)), dma((CHUNKS, PEERS)), dma((2, CHUNKS)), dma((CHUNKS, PEERS)), dma((CHUNKS, PEERS)),
            dma((CHUNKS, PEERS)), dma((CHUNKS, PEERS)), dma((2,)), dma, dma((PEERS,)), dma((PEERS,)),
            dma((2,)), dma((PEERS,)), dma((PEERS,)), dma((PEERS,)), dma((PEERS,)),
        ],
        compiler_params=pltpu.CompilerParams(collective_id=0, has_side_effects=True, vmem_limit_bytes=56 * 2**20),
    )(features[0], packed, long_filter, out_weight, *matrices)
    return result[None]


def solution(mesh):
    placed = (P("fsdp", "ctx", None), P(None, "fsdp"), P(), P(None, "fsdp"))
    return jax.shard_map(
        shards, mesh=mesh, in_specs=placed, out_specs=P("fsdp", "ctx", None), check_vma=False
    )
```

time: 840 us -> 144 us (0.17); the launches traced: 823 us -> 142 us
  local copies, waits for them, and re-layouts: 425 us -> 3 us
  waiting for transfers between devices: 225 us -> 0 us
  Pallas kernels: 0 us -> 138 us
  blocking collectives: 58.2 us -> 0 us
  matrix products: 51.1 us -> 0 us
  other arithmetic: 38.4 us -> 0.6 us
  between operations: 13.6 us -> 0.01 us
  starting transfers between devices: 12.6 us -> 0 us
    gather x10 -> x0, local copies, waits for them, and re-layouts: 413 us -> none  [toeplitz_block(): return jnp.take(filter_rows, position, axis=1)]
    all_gather x1 -> x0, waiting for transfers between devices: 179 us -> none  [shards(): lax.all_gather(gated, 'fsdp', axis=0, tiled=True)]
    pallas_call x0 -> x1, Pallas kernels: none -> 138 us  [shards(): pl.pallas_call(mixer_kernel, name='mixer', out_shape=jax.ShapeDtypeStruct...]
    dot_general x6 -> x0, matrix products: 51.1 us -> none  [the longest x5 42.6 us: block_term(): jnp.einsum('fts,fgs->fgt', matrix, block, preferred_element_type=jnp.floa...]
    ppermute x5 -> x0, waiting for transfers between devices: 45.2 us -> none  [passed_along(): return lax.ppermute(array, axis, pairs)]
    all_gather x1 -> x0, blocking collectives: 33.1 us -> none  [shards(): lax.all_gather(short_weight, 'fsdp', axis=1, tiled=True).astype(jnp.float32)]
    all_to_all x1 -> x0, blocking collectives: 25 us -> none  [shards(): lax.all_to_all(projected, 'fsdp', split_axis=0, concat_axis=1, tiled=True)]
    add x5 -> x0, other arithmetic: 24.6 us -> none  [the longest x1 24.6 us: shards(): filtered = filtered + tap_full[tap_index] * extended[begin:begin + rows]]
  transfers between devices with their start and end apart: 6 -> 0, of which waited for: 4 -> 0; matrix products, arithmetic and copies ran while one was open for 55% -> 0% of each run, Pallas kernels for 0% -> 0%
where the time goes in v1:
time: 144 us; the launch traced here: 142 us
  Pallas kernels  138 us (96%)
  local copies, waits for them, and re-layouts  3 us (2%)
    pallas_call x1, Pallas kernels, shards(): pl.pallas_call(mixer_kernel, name='mixer', out_shape=jax.ShapeDtypeStruct...  138 us

profile of v1, /device:TPU:16, one launch (start us, length us, event | category | flops | bytes accessed | tf_op | source)
XLA Modules:
  0.0 141.8 jit_solution(18220082556099483880)
XLA Ops:
  0.0 0.7 pad_slice_fusion.1
  0.7 0.6 pad_maximum_fusion.taps_in
  1.3 138.2 %mixer.1 = bf16[128,4096]{1,0:T(8,128)(2,1)} custom-call(bf16[128,12288]{1,0:T(8,128)(2,1)} %bitcast.3, bf16[16,384]{1,0:T(8,128)(2,1)} %pad_maximum_fusion.taps_in, bf16[512,256]{1,0:T(8,128)(2,1)} %filt.1, bf16[4096,256]{1,0:T(8,128)(2,1)} %weight.1, bf16[1024,512]{1,0:T(8,128)(2,1)} %constant.11.clone.fwd_hi_in, ...), custom_call_target="tpu_custom_call" | custom-call | tf_op jit(solution)/shard_map/mixer/pallas_call | solution.py:440
  139.5 2.3 %copy.10 = bf16[1,128,4096]{2,1,0:T(8,128)(2,1)} copy(bf16[1,128,4096]{2,1,0:T(8,128)(2,1)} %bitcast.2) | data formatting | bytes 2097152

commit v2 on v1

v2 whole, which is shorter than its diff:
```python
import functools

import jax
import jax.numpy as jnp
import ml_dtypes
import numpy as np
from jax import lax
from jax.experimental import pallas as pl
from jax.experimental.pallas import tpu as pltpu
from jax.sharding import PartitionSpec as P

MESH = pl.DeviceIdType.MESH
BF16 = jnp.bfloat16
F32 = jnp.float32

ROWS = 128
CHANNELS = 4096
FILTERS = 256
TAPS = 7
SPAN = 512
HALO = 8
PEERS = 4
CHUNKS = 8
GROUPS = 4
WIDTH = CHANNELS // (PEERS * CHUNKS)
CHUNK = PEERS * WIDTH
GROUP = CHANNELS // GROUPS
HALF = GROUP // 2
NEAR = 8
SHARDS = 16
COLS = CHANNELS // SHARDS
OUT = PEERS * COLS
TAPCOLS = 3 * CHANNELS // SHARDS


def transform_matrices():
    order = np.concatenate([np.arange(0, SPAN, 2), np.arange(1, SPAN, 2)])
    turns = (np.outer(2 * order + 1, np.arange(SPAN)) % (4 * SPAN)) * (2 * np.pi / (4 * SPAN))
    forward = np.concatenate([np.cos(turns), -np.sin(turns)], axis=0)
    high = forward.astype(ml_dtypes.bfloat16)
    low = (forward - high.astype(np.float64)).astype(ml_dtypes.bfloat16)
    scale = np.float64(1.0 / SPAN)
    back_high = (high.astype(np.float64).T * scale).astype(ml_dtypes.bfloat16)
    back_low = (low.astype(np.float64).T * scale).astype(ml_dtypes.bfloat16)
    return high, low, back_high, back_low


def dot(a, b):
    return jnp.dot(a, b, preferred_element_type=F32)


def mixer_kernel(
    feat, taps_in, filt, weight, fwd_hi_in, fwd_lo_in, inv_hi_in, inv_lo_in,
    out,
    ext, tail, halo_out, halo_in, halo, taps_all, taps, fwd_hi, fwd_lo, inv_hi, inv_lo, spec, y_hi, y_lo,
    prod, cur, prev, convs, back, gated, wts, acc, outs,
    local_sem, halo_send, halo_recv, tap_send, tap_recv, zf_send, zf_recv, yf_sem, zb_send, zb_recv,
    xg_send, xg_recv, xr_send, xr_recv, wz_send, wz_recv, wy_send, wy_recv, wm_sem, wc_send, wc_recv, o_send, o_recv,
):
    ctx, fsdp = lax.axis_index("ctx"), lax.axis_index("fsdp")
    y, zl = ctx // 4, ctx % 4
    x, zh, core = fsdp // 4, (fsdp // 2) % 2, fsdp % 2
    slot = zh * 2 + core
    far_slot = (1 - zh) * 2 + core
    far_shard = x * 4 + far_slot

    def device(y_=y, zl_=zl, x_=x, zh_=zh, core_=core):
        return (y_ * 4 + zl_, (x_ * 2 + zh_) * 2 + core_)

    def remote(src, dst, send, recv, to):
        return pltpu.make_async_remote_copy(
            src_ref=src, dst_ref=dst, send_sem=send, recv_sem=recv, device_id=to, device_id_type=MESH
        )

    def ring(k, at):
        return lax.rem(at + k, PEERS)

    def features_load(part, at):
        lanes = pl.ds(part * CHANNELS, CHANNELS)
        return pltpu.make_async_copy(feat.at[:, lanes], ext.at[:, lanes], local_sem.at[at])

    tail_load = pltpu.make_async_copy(feat.at[pl.ds(ROWS - 16, 16)], tail, local_sem.at[9])
    tail_load.start()
    loads = [
        features_load(1, 0),
        features_load(2, 1),
        pltpu.make_async_copy(fwd_hi_in, fwd_hi, local_sem.at[2]),
        pltpu.make_async_copy(fwd_lo_in, fwd_lo, local_sem.at[3]),
        features_load(0, 4),
        pltpu.make_async_copy(inv_hi_in, inv_hi, local_sem.at[5]),
        pltpu.make_async_copy(inv_lo_in, inv_lo, local_sem.at[6]),
        pltpu.make_async_copy(weight, wts.at[slot], local_sem.at[7]),
    ]
    for load in loads:
        load.start()

    barrier = pltpu.get_barrier_semaphore()

    def greet(to):
        pl.semaphore_signal(barrier, inc=1, device_id=to, device_id_type=MESH)

    def near(k):
        other = lax.rem(x * 2 + core + k, NEAR)
        return other // 2, lax.rem(other, 2)

    def greet_near(k, carry):
        x_, core_ = near(k)
        greet(device(x_=x_, core_=core_))
        return carry

    lax.fori_loop(1, NEAR, greet_near, 0)
    for k in range(1, PEERS):
        greet(device(zl_=ring(k, zl)))
        greet(device(y_=ring(k, y)))
    after, before = lax.rem(ctx + 1, 16), lax.rem(ctx + 15, 16)
    greet((after, fsdp))
    greet((before, fsdp))
    greet(device(zh_=1 - zh))
    greet(device(zl_=3 - zl, zh_=1 - zh))
    greet(device(zl_=ring(2, zl), zh_=1 - zh))

    own_taps = jnp.concatenate([taps_in[...].astype(F32), jnp.zeros((8 - TAPS, TAPCOLS), F32)], axis=0)
    own_taps = jnp.concatenate([own_taps[:, : TAPCOLS // 2], own_taps[:, TAPCOLS // 2 :]], axis=0)
    taps_all[fsdp] = own_taps.astype(BF16)

    tail_load.wait()

    def pack(part, group):
        rows = tail[:, part * CHANNELS + group * GROUP : part * CHANNELS + (group + 1) * GROUP].astype(F32)[16 - HALO :]
        packed = jnp.concatenate([rows[:, :HALF], rows[:, HALF:]], axis=0)
        return packed.astype(BF16)

    for group in range(GROUPS):
        halo_out[group, 0] = pack(1, group)
        halo_out[group, 1] = pack(2, group)
        halo_out[GROUPS + group // 2, group % 2] = pack(0, group)

    pl.semaphore_wait(barrier, NEAR - 1 + 2 * (PEERS - 1) + 5)

    far_taps = remote(taps_all.at[fsdp], taps_all.at[fsdp], tap_send.at[0, 0], tap_recv.at[fsdp], device(zh_=1 - zh))
    far_taps.start()

    def tap_copy(k, zh_):
        x_, core_ = near(k)
        shard = x * 4 + zh_ * 2 + core
        return remote(taps_all.at[shard], taps_all.at[shard], tap_send.at[zh_, k], tap_recv.at[shard], device(x_=x_, core_=core_))

    def tap_arrival(k, zh_):
        x_, core_ = near(k)
        shard = x_ * 4 + zh_ * 2 + core_
        return remote(taps_all.at[shard], taps_all.at[shard], tap_send.at[zh_, k], tap_recv.at[shard], device(x_=x_, core_=core_))

    def start_taps(k, carry):
        tap_copy(k, zh).start()
        return carry

    lax.fori_loop(1, NEAR, start_taps, 0)

    def halo_copy(at):
        return remote(halo_out.at[at], halo_in.at[at], halo_send.at[at], halo_recv.at[at], (after, fsdp))

    for group in range(GROUPS):
        halo_copy(group).start()

    def quarter(ref, which):
        return ref.at[pl.ds(pl.multiple_of(which * GROUP, GROUP), GROUP)]

    mate = device(core_=1 - core)
    mate_copy = remote(weight, wts.at[slot], wm_sem.at[0], wm_sem.at[1], mate)
    mate_copy.start()

    def far_copy(j, to_zl):
        return remote(quarter(weight, y), quarter(wts.at[slot], y), wz_send.at[j], wz_recv, device(zl_=to_zl, zh_=1 - zh))

    @pl.when(zl == 0)
    def _():
        far_copy(1, 2).start()
        far_copy(0, 3).start()

    @pl.when(zl == 3)
    def _():
        far_copy(1, 1).start()
        far_copy(0, 0).start()

    remote(taps_all.at[far_shard], taps_all.at[far_shard], tap_send.at[0, 0], tap_recv.at[far_shard], device(zh_=1 - zh)).wait_recv()

    def pass_taps(k, carry):
        tap_copy(k, 1 - zh).start()
        return carry

    lax.fori_loop(1, NEAR, pass_taps, 0)

    loads[2].wait()
    loads[3].wait()
    mine_filt = filt[:, pl.ds(pl.multiple_of(lax.rem(zl, FILTERS // WIDTH) * WIDTH, WIDTH), WIDTH)]
    for part in range(4):
        rows = pl.ds(part * 256, 256)
        spec[rows, :] = dot(fwd_hi[rows, :], mine_filt) + dot(fwd_lo[rows, :], mine_filt)

    @pl.when(y == 0)
    def _():
        prev[...] = jnp.zeros(prev.shape, BF16)

    loads[0].wait()
    loads[1].wait()
    loads[4].wait()

    def wait_taps(k, carry):
        tap_arrival(k, 0).wait_recv()
        tap_arrival(k, 1).wait_recv()
        return carry

    lax.fori_loop(1, NEAR, wait_taps, 0)
    for shard in range(SHARDS):
        block = taps_all[shard].astype(F32)
        taps[:, pl.ds(shard * TAPCOLS, TAPCOLS // 2)] = block[:8]
        taps[:, pl.ds(shard * TAPCOLS + TAPCOLS // 2, TAPCOLS // 2)] = block[8:]

    keep = jnp.where(ctx > 0, 1.0, 0.0).astype(F32)

    def unpack(at, which, begin):
        block = halo_in[at, which].astype(F32) * keep
        halo[:, pl.ds(pl.multiple_of(begin, HALF), HALF)] = block[:HALO]
        halo[:, pl.ds(pl.multiple_of(begin + HALF, HALF), HALF)] = block[HALO:]

    def short_filter(begin):
        columns = pl.ds(pl.multiple_of(begin, 128), 128)
        rows = jnp.concatenate([halo[:, columns], ext[:, columns].astype(F32)], axis=0)
        weights = taps[:, columns]
        total = weights[0:1] * rows[HALO:]
        for lag in range(1, TAPS):
            total = total + weights[lag : lag + 1] * pltpu.roll(rows, lag, 0)[HALO:]
        return total

    def own_rows(which):
        return pl.ds(pl.multiple_of(which * ROWS, ROWS), ROWS)

    def zf_copy(i, k):
        q = ring(k, zl)
        return remote(prod.at[i, q], cur.at[i, own_rows(zl)], zf_send.at[i, k], zf_recv.at[i, zl], device(zl_=q))

    def zf_arrival(i, k):
        q = ring(k, zl)
        return remote(prod.at[i, q], cur.at[i, own_rows(q)], zf_send.at[i, k], zf_recv.at[i, q], device(zl_=q))

    def products(i):
        group = i // 2

        @pl.when(lax.rem(i, 2) == 0)
        def _():
            halo_copy(group).wait_recv()
            unpack(group, 0, CHANNELS + group * GROUP)
            unpack(group, 1, 2 * CHANNELS + group * GROUP)

        def one(q, inner):
            begin = i * CHUNK + q * WIDTH
            keys = short_filter(CHANNELS + begin)
            values = short_filter(2 * CHANNELS + begin)
            prod[i, q] = (keys * values).astype(BF16)
            return inner

        lax.fori_loop(0, PEERS, one, 0)
        for k in range(1, PEERS):
            zf_copy(i, k).start()
        cur[i, own_rows(zl), :] = prod[i, zl]

        @pl.when(i == 1)
        def _():
            for at in (GROUPS, GROUPS + 1):
                halo_copy(at).start()


    def yf_copy(i):
        return remote(cur.at[i], prev.at[i], yf_sem.at[0, i], yf_sem.at[1, i], device(y_=ring(1, y)))

    def onward(i):
        for k in range(1, PEERS):
            zf_arrival(i, k).wait_recv()

        @pl.when(y < PEERS - 1)
        def _():
            yf_copy(i).start()

    def zb_copy(i, k):
        q = ring(k, zl)
        return remote(convs.at[i, own_rows(q)], back.at[i, zl], zb_send.at[i, k], zb_recv.at[i, zl], device(zl_=q))

    def zb_arrival(i, k):
        q = ring(k, zl)
        return remote(convs.at[i, own_rows(q)], back.at[i, q], zb_send.at[i, k], zb_recv.at[i, q], device(zl_=q))

    def convolve(i):
        @pl.when(y > 0)
        def _():
            yf_copy(i).wait_recv()

        def frequencies(part, carry):
            real = pl.ds(pl.multiple_of(part * 128, 128), 128)
            imag = pl.ds(pl.multiple_of(SPAN + part * 128, 128), 128)
            both = jnp.concatenate([cur[i], prev[i]], axis=1)
            re = dot(fwd_hi[real, :], both) + dot(fwd_lo[real, :], both)
            im = dot(fwd_hi[imag, :], both) + dot(fwd_lo[imag, :], both)
            sign = jnp.where(part < 2, 1.0, -1.0).astype(F32)
            a = re[:, :WIDTH] - sign * im[:, WIDTH:]
            b = im[:, :WIDTH] + sign * re[:, WIDTH:]
            hr, hi = spec[real, :], spec[imag, :]
            yr = hr * a - hi * b
            yi = hr * b + hi * a
            yr_hi, yi_hi = yr.astype(BF16), yi.astype(BF16)
            y_hi[real, :] = yr_hi
            y_hi[imag, :] = yi_hi
            y_lo[real, :] = (yr - yr_hi.astype(F32)).astype(BF16)
            y_lo[imag, :] = (yi - yi_hi.astype(F32)).astype(BF16)
            return carry

        lax.fori_loop(0, 4, frequencies, 0)

        def positions(part, carry):
            rows = own_rows(part)
            both = dot(inv_hi[rows, :], jnp.concatenate([y_hi[...], y_lo[...]], axis=1))
            got = both[:, :WIDTH] + both[:, WIDTH:] + dot(inv_lo[rows, :], y_hi[...])
            convs[i, rows, :] = got.astype(BF16)
            return carry

        lax.fori_loop(0, PEERS, positions, 0)
        for k in range(1, PEERS):
            zb_copy(i, k).start()
        back[i, zl] = convs[i, own_rows(zl), :]

    left, right = ring(3, x), ring(1, x)

    def xg_copy(i, to, at):
        return remote(gated.at[i, x], gated.at[i, x], xg_send.at[i, at], xg_recv.at[i, x], device(x_=to))

    def xg_arrival(i, source, at):
        return remote(gated.at[i, source], gated.at[i, source], xg_send.at[i, at], xg_recv.at[i, source], device(x_=source))

    def xr_copy(i, source, to, at):
        ref = gated.at[i, source, pl.ds(at * (ROWS // 2), ROWS // 2)]
        return remote(ref, ref, xr_send.at[i, at], xr_recv.at[i, at], device(x_=to))

    def gate(i):
        @pl.when(i == 0)
        def _():
            for at in (GROUPS, GROUPS + 1):
                halo_copy(at).wait_recv()
            for group in range(GROUPS):
                unpack(GROUPS + group // 2, group % 2, group * GROUP)

        for k in range(1, PEERS):
            zb_arrival(i, k).wait_recv()
        for q in range(PEERS):
            query = short_filter(i * CHUNK + q * WIDTH)
            gated[i, x, :, q * WIDTH : (q + 1) * WIDTH] = (query * back[i, q].astype(F32)).astype(BF16)
        xg_copy(i, right, 0).start()
        xg_copy(i, left, 1).start()

    def relay(i):
        xg_arrival(i, left, 0).wait_recv()
        xr_copy(i, left, right, 0).start()
        xg_arrival(i, right, 1).wait_recv()
        xr_copy(i, right, left, 1).start()

    def far_arrivals(i):
        across = ring(2, x)
        xr_copy(i, across, left, 0).wait_recv()
        xr_copy(i, across, right, 1).wait_recv()

    def project(group):
        far_arrivals(2 * group)
        far_arrivals(2 * group + 1)
        lhs = [gated[2 * group + part].reshape(PEERS * ROWS, CHUNK) for part in range(2)]

        def block(j, carry):
            term = acc[j]
            for part in range(2):
                term = term + dot(lhs[part], wts[j, pl.ds(pl.multiple_of(group * GROUP + part * CHUNK, CHUNK), CHUNK), :])
            acc[j] = term
            return carry

        lax.fori_loop(0, PEERS, block, 0)

    def wy_copy(k):
        ref = quarter(wts.at[far_slot], ring(k, y))
        return remote(ref, ref, wy_send.at[k], wy_recv.at[k], device(y_=ring(3, y)))

    def wy_arrival(k):
        ref = quarter(wts.at[far_slot], ring(k + 1, y))
        return remote(ref, ref, wy_send.at[k], wy_recv.at[k], device(y_=ring(1, y)))

    def wc_copy(which):
        ref = quarter(wts.at[far_slot], which)
        return remote(ref, ref, wc_send.at[which], wc_recv.at[which], mate)

    def wc_arrival(which):
        ref = quarter(wts.at[(1 - zh) * 2 + 1 - core], which)
        return remote(ref, ref, wc_send.at[which], wc_recv.at[which], mate)

    def columns_first():
        far = quarter(wts.at[far_slot], y)
        remote(far, far, wz_send.at[0], wz_recv, device(zl_=3 - zl, zh_=1 - zh)).wait_recv()
        wy_copy(0).start()
        wc_copy(y).start()

    def columns_next(k):
        wy_arrival(k - 1).wait_recv()

        @pl.when(k < PEERS - 1)
        def _():
            wy_copy(k).start()

        wc_copy(ring(k, y)).start()

    def columns_last():
        loads[7].wait()
        mate_copy.wait_recv()
        for which in range(PEERS):
            wc_arrival(which).wait_recv()

    loads[5].wait()
    loads[6].wait()
    acc[...] = jnp.zeros(acc.shape, F32)

    def step(t, carry):
        @pl.when(t < CHUNKS)
        def _():
            products(t)

        @pl.when(jnp.logical_and(t >= 2, t < CHUNKS + 2))
        def _():
            onward(t - 2)

        @pl.when(jnp.logical_and(t >= 3, t < CHUNKS + 3))
        def _():
            convolve(t - 3)

        @pl.when(jnp.logical_and(t >= 4, t < CHUNKS + 4))
        def _():
            gate(t - 4)

        @pl.when(t >= 5)
        def _():
            relay(t - 5)

        @pl.when(t == 4)
        def _():
            columns_first()

        @pl.when(jnp.logical_or(t == 6, jnp.logical_or(t == 8, t == 10)))
        def _():
            columns_next(t // 2 - 2)

        @pl.when(t == 10)
        def _():
            columns_last()

        @pl.when(t >= 10)
        def _():
            project(t - 10)

        return carry

    lax.fori_loop(0, CHUNKS + 5, step, 0)

    mine = pl.ds(pl.multiple_of(x * OUT, OUT), OUT)

    def out_copy(k):
        q = ring(k, x)
        return remote(outs.at[q], out.at[:, mine], o_send.at[k], o_recv.at[x], device(x_=q))

    def out_arrival(k):
        q = ring(k, x)
        return remote(outs.at[q], out.at[:, pl.ds(pl.multiple_of(q * OUT, OUT), OUT)], o_send.at[k], o_recv.at[q], device(x_=q))

    last = GROUPS - 1
    far_arrivals(2 * last)
    far_arrivals(2 * last + 1)

    def finish(k, carry):
        q = ring(k, x)
        lhs = jnp.concatenate([gated[2 * last, q], gated[2 * last + 1, q]], axis=1)
        for j in range(PEERS):
            total = acc[j, own_rows(q), :] + dot(lhs, wts[j, last * GROUP :, :])
            outs[q, :, j * COLS : (j + 1) * COLS] = total.astype(BF16)

        @pl.when(k < PEERS)
        def _():
            out_copy(k).start()

        return carry

    lax.fori_loop(1, PEERS + 1, finish, 0)
    own = pltpu.make_async_copy(outs.at[x], out.at[:, mine], local_sem.at[8])
    own.start()
    own.wait()
    for k in range(1, PEERS):
        out_arrival(k).wait_recv()

    far_taps.wait_send()
    mate_copy.wait_send()
    for at in range(GROUPS + 2):
        halo_copy(at).wait_send()

    def sent_taps(k, carry):
        tap_copy(k, 0).wait_send()
        tap_copy(k, 1).wait_send()
        return carry

    lax.fori_loop(1, NEAR, sent_taps, 0)

    @pl.when(jnp.logical_or(zl == 0, zl == 3))
    def _():
        far_copy(0, 3 - zl).wait_send()
        far_copy(1, ring(2, zl)).wait_send()

    for k in range(1, PEERS):
        wy_copy(k - 1).wait_send()
        out_copy(k).wait_send()
    for which in range(PEERS):
        wc_copy(which).wait_send()

    def sent_chunk(i, carry):
        for k in range(1, PEERS):
            zf_copy(i, k).wait_send()
            zb_copy(i, k).wait_send()
        xg_copy(i, right, 0).wait_send()
        xg_copy(i, left, 1).wait_send()
        xr_copy(i, left, right, 0).wait_send()
        xr_copy(i, right, left, 1).wait_send()

        @pl.when(y < PEERS - 1)
        def _():
            yf_copy(i).wait_send()

        return carry

    lax.fori_loop(0, CHUNKS, sent_chunk, 0)


def shards(features, short_weight, long_filter, out_weight):
    matrices = [jnp.asarray(m) for m in transform_matrices()]
    anywhere = pl.BlockSpec(memory_space=pl.ANY)
    dma = pltpu.SemaphoreType.DMA
    result = pl.pallas_call(
        mixer_kernel,
        name="mixer",
        out_shape=jax.ShapeDtypeStruct((ROWS, CHANNELS), BF16),
        in_specs=[anywhere, pl.BlockSpec(memory_space=pltpu.VMEM), pl.BlockSpec(memory_space=pltpu.VMEM)] + [anywhere] * 5,
        out_specs=anywhere,
        scratch_shapes=[
            pltpu.VMEM((ROWS, 3 * CHANNELS), BF16),
            pltpu.VMEM((16, 3 * CHANNELS), BF16),
            pltpu.VMEM((GROUPS + 2, 2, 2 * HALO, HALF), BF16),
            pltpu.VMEM((GROUPS + 2, 2, 2 * HALO, HALF), BF16),
            pltpu.VMEM((HALO, 3 * CHANNELS), F32),
            pltpu.VMEM((SHARDS, 16, TAPCOLS // 2), BF16),
            pltpu.VMEM((8, 3 * CHANNELS), F32),
            pltpu.VMEM((2 * SPAN, SPAN), BF16),
            pltpu.VMEM((2 * SPAN, SPAN), BF16),
            pltpu.VMEM((SPAN, 2 * SPAN), BF16),
            pltpu.VMEM((SPAN, 2 * SPAN), BF16),
            pltpu.VMEM((2 * SPAN, WIDTH), F32),
            pltpu.VMEM((2 * SPAN, WIDTH), BF16),
            pltpu.VMEM((2 * SPAN, WIDTH), BF16),
            pltpu.VMEM((CHUNKS, PEERS, ROWS, WIDTH), BF16),
            pltpu.VMEM((CHUNKS, SPAN, WIDTH), BF16),
            pltpu.VMEM((CHUNKS, SPAN, WIDTH), BF16),
            pltpu.VMEM((CHUNKS, SPAN, WIDTH), BF16),
            pltpu.VMEM((CHUNKS, PEERS, ROWS, WIDTH), BF16),
            pltpu.VMEM((CHUNKS, PEERS, ROWS, CHUNK), BF16),
            pltpu.VMEM((PEERS, CHANNELS, COLS), BF16),
            pltpu.VMEM((PEERS, PEERS * ROWS, COLS), F32),
            pltpu.VMEM((PEERS, ROWS, OUT), BF16),
            dma((10,)), dma((GROUPS + 2,)), dma((GROUPS + 2,)), dma((2, NEAR)), dma((SHARDS,)),
            dma((CHUNKS, PEERS)), dma((CHUNKS, PEERS)), dma((2, CHUNKS)), dma((CHUNKS, PEERS)), dma((CHUNKS, PEERS)),
            dma((CHUNKS, 2)), dma((CHUNKS, PEERS)), dma((CHUNKS, 2)), dma((CHUNKS, 2)),
            dma((2,)), dma, dma((PEERS,)), dma((PEERS,)), dma((2,)), dma((PEERS,)), dma((PEERS,)), dma((PEERS,)), dma((PEERS,)),
        ],
        compiler_params=pltpu.CompilerParams(collective_id=0, has_side_effects=True, vmem_limit_bytes=56 * 2**20),
    )(features[0], short_weight, long_filter, out_weight, *matrices)
    return result[None]


def solution(mesh):
    placed = (P("fsdp", "ctx", None), P(None, "fsdp"), P(), P(None, "fsdp"))
    return jax.shard_map(
        shards, mesh=mesh, in_specs=placed, out_specs=P("fsdp", "ctx", None), check_vma=False
    )
```

time: 144 us -> 113 us (0.78)
  the two profiles are of different devices: /device:TPU:16 before, /device:TPU:1 now
where the time goes in v2:
time: 113 us
  Pallas kernels  110 us (97%)
  local copies, waits for them, and re-layouts  2.29 us (2%)
    pallas_call x1, Pallas kernels, shards(): pl.pallas_call(mixer_kernel, name='mixer', out_shape=jax.ShapeDtypeStruct...  110 us
    unnamed x1, local copies, waits for them, and re-layouts  2.29 us

profile of v2, /device:TPU:1, one launch (start us, length us, event | category | flops | bytes accessed | tf_op | source)
XLA Modules:
  0.0 112.6 jit_solution(12413163293303218395)
XLA Ops:
  0.0 110.3 %mixer.1 = bf16[128,4096]{1,0:T(8,128)(2,1)} custom-call(bf16[128,12288]{1,0:T(8,128)(2,1)} %bitcast.3, bf16[7,768]{1,0:T(8,128)(2,1)} %taps_in.1, bf16[512,256]{1,0:T(8,128)(2,1)} %filt.1, bf16[4096,256]{1,0:T(8,128)(2,1)} %weight.1, bf16[1024,512]{1,0:T(8,128)(2,1)} %constant.8.clone.fwd_hi_in, bf16[1024,512]{1,0:T(8,128)(2,1)} %constant.9.clone.fwd_lo_in, ...), custom_call_target="tpu_custom_call" | custom-call | tf_op jit(solution)/shard_map/mixer/pallas_call | solution.py:544
  110.3 2.3 %copy.10 = bf16[1,128,4096]{2,1,0:T(8,128)(2,1)} copy(bf16[1,128,4096]{2,1,0:T(8,128)(2,1)} %bitcast.2) | data formatting | bytes 2097152

commit v3 on v2

--- a/solution.py
+++ b/solution.py
@@ -50,19 +50,19 @@
 
 
 def mixer_kernel(
-    feat, taps_in, filt, weight, fwd_hi_in, fwd_lo_in, inv_hi_in, inv_lo_in,
+    feat, taps_in, filt_in, weight, fwd_hi_in, fwd_lo_in, inv_hi_in, inv_lo_in,
     out,
-    ext, tail, halo_out, halo_in, halo, taps_all, taps, fwd_hi, fwd_lo, inv_hi, inv_lo, spec, y_hi, y_lo,
+    ext, tail, filt, halo_out, halo_in, halo, taps_all, taps, fwd_hi, fwd_lo, inv_hi, inv_lo, spec, y_hi, y_lo,
     prod, cur, prev, convs, back, gated, wts, acc, outs,
-    local_sem, halo_send, halo_recv, tap_send, tap_recv, zf_send, zf_recv, yf_sem, zb_send, zb_recv,
-    xg_send, xg_recv, xr_send, xr_recv, wz_send, wz_recv, wy_send, wy_recv, wm_sem, wc_send, wc_recv, o_send, o_recv,
+    local_sem, halo_send, halo_recv, wt_send, wt_recv, tap_send, tap_recv, zf_send, zf_recv, yf_sem, zb_send, zb_recv,
+    xg_send, xg_recv, xr_send, xr_recv, wz_send, wz_recv, wy_send, wy_recv, wm_sem, wc_send, wc_recv, o_send, o_recv, own_sem,
 ):
     ctx, fsdp = lax.axis_index("ctx"), lax.axis_index("fsdp")
     y, zl = ctx // 4, ctx % 4
     x, zh, core = fsdp // 4, (fsdp // 2) % 2, fsdp % 2
     slot = zh * 2 + core
     far_slot = (1 - zh) * 2 + core
-    far_shard = x * 4 + far_slot
+    here = x * 2 + core
 
     def device(y_=y, zl_=zl, x_=x, zh_=zh, core_=core):
         return (y_ * 4 + zl_, (x_ * 2 + zh_) * 2 + core_)
@@ -90,6 +90,7 @@
         pltpu.make_async_copy(inv_hi_in, inv_hi, local_sem.at[5]),
         pltpu.make_async_copy(inv_lo_in, inv_lo, local_sem.at[6]),
         pltpu.make_async_copy(weight, wts.at[slot], local_sem.at[7]),
+        pltpu.make_async_copy(filt_in, filt, local_sem.at[10]),
     ]
     for load in loads:
         load.start()
@@ -115,13 +116,12 @@
     after, before = lax.rem(ctx + 1, 16), lax.rem(ctx + 15, 16)
     greet((after, fsdp))
     greet((before, fsdp))
-    greet(device(zh_=1 - zh))
     greet(device(zl_=3 - zl, zh_=1 - zh))
     greet(device(zl_=ring(2, zl), zh_=1 - zh))
 
     own_taps = jnp.concatenate([taps_in[...].astype(F32), jnp.zeros((8 - TAPS, TAPCOLS), F32)], axis=0)
     own_taps = jnp.concatenate([own_taps[:, : TAPCOLS // 2], own_taps[:, TAPCOLS // 2 :]], axis=0)
-    taps_all[fsdp] = own_taps.astype(BF16)
+    taps_all[here, zh] = own_taps.astype(BF16)
 
     tail_load.wait()
 
@@ -135,26 +135,30 @@
         halo_out[group, 1] = pack(2, group)
         halo_out[GROUPS + group // 2, group % 2] = pack(0, group)
 
-    pl.semaphore_wait(barrier, NEAR - 1 + 2 * (PEERS - 1) + 5)
-
-    far_taps = remote(taps_all.at[fsdp], taps_all.at[fsdp], tap_send.at[0, 0], tap_recv.at[fsdp], device(zh_=1 - zh))
-    far_taps.start()
-
-    def tap_copy(k, zh_):
+    pl.semaphore_wait(barrier, NEAR - 1 + 2 * (PEERS - 1) + 4)
+
+    def far_taps(j, to_zl):
+        ref = taps_all.at[here, zh]
+        return remote(ref, ref, wt_send.at[j], wt_recv, device(zl_=to_zl, zh_=1 - zh))
+
+    @pl.when(zl == 0)
+    def _():
+        far_taps(1, 2).start()
+        far_taps(0, 3).start()
+
+    @pl.when(zl == 3)
+    def _():
+        far_taps(1, 1).start()
+        far_taps(0, 0).start()
+
+    def tap_copy(k):
         x_, core_ = near(k)
-        shard = x * 4 + zh_ * 2 + core
-        return remote(taps_all.at[shard], taps_all.at[shard], tap_send.at[zh_, k], tap_recv.at[shard], device(x_=x_, core_=core_))
-
-    def tap_arrival(k, zh_):
+        return remote(taps_all.at[here], taps_all.at[here], tap_send.at[k], tap_recv.at[here], device(x_=x_, core_=core_))
+
+    def tap_arrival(k):
         x_, core_ = near(k)
-        shard = x_ * 4 + zh_ * 2 + core_
-        return remote(taps_all.at[shard], taps_all.at[shard], tap_send.at[zh_, k], tap_recv.at[shard], device(x_=x_, core_=core_))
-
-    def start_taps(k, carry):
-        tap_copy(k, zh).start()
-        return carry
-
-    lax.fori_loop(1, NEAR, start_taps, 0)
+        there = x_ * 2 + core_
+        return remote(taps_all.at[there], taps_all.at[there], tap_send.at[k], tap_recv.at[there], device(x_=x_, core_=core_))
 
     def halo_copy(at):
         return remote(halo_out.at[at], halo_in.at[at], halo_send.at[at], halo_recv.at[at], (after, fsdp))
@@ -162,12 +166,16 @@
     for group in range(GROUPS):
         halo_copy(group).start()
 
+    ref = taps_all.at[here, 1 - zh]
+    remote(ref, ref, wt_send.at[0], wt_recv, device(zl_=3 - zl, zh_=1 - zh)).wait_recv()
+    for k in (4, 3, 5, 2, 6, 1, 7):
+        tap_copy(k).start()
+
     def quarter(ref, which):
         return ref.at[pl.ds(pl.multiple_of(which * GROUP, GROUP), GROUP)]
 
     mate = device(core_=1 - core)
     mate_copy = remote(weight, wts.at[slot], wm_sem.at[0], wm_sem.at[1], mate)
-    mate_copy.start()
 
     def far_copy(j, to_zl):
         return remote(quarter(weight, y), quarter(wts.at[slot], y), wz_send.at[j], wz_recv, device(zl_=to_zl, zh_=1 - zh))
@@ -182,16 +190,9 @@
         far_copy(1, 1).start()
         far_copy(0, 0).start()
 
-    remote(taps_all.at[far_shard], taps_all.at[far_shard], tap_send.at[0, 0], tap_recv.at[far_shard], device(zh_=1 - zh)).wait_recv()
-
-    def pass_taps(k, carry):
-        tap_copy(k, 1 - zh).start()
-        return carry
-
-    lax.fori_loop(1, NEAR, pass_taps, 0)
-
     loads[2].wait()
     loads[3].wait()
+    loads[8].wait()
     mine_filt = filt[:, pl.ds(pl.multiple_of(lax.rem(zl, FILTERS // WIDTH) * WIDTH, WIDTH), WIDTH)]
     for part in range(4):
         rows = pl.ds(part * 256, 256)
@@ -205,14 +206,10 @@
     loads[1].wait()
     loads[4].wait()
 
-    def wait_taps(k, carry):
-        tap_arrival(k, 0).wait_recv()
-        tap_arrival(k, 1).wait_recv()
-        return carry
-
-    lax.fori_loop(1, NEAR, wait_taps, 0)
+    for k in range(1, NEAR):
+        tap_arrival(k).wait_recv()
     for shard in range(SHARDS):
-        block = taps_all[shard].astype(F32)
+        block = taps_all[shard // 4 * 2 + shard % 2, shard // 2 % 2].astype(F32)
         taps[:, pl.ds(shard * TAPCOLS, TAPCOLS // 2)] = block[:8]
         taps[:, pl.ds(shard * TAPCOLS + TAPCOLS // 2, TAPCOLS // 2)] = block[8:]
 
@@ -329,14 +326,19 @@
 
     left, right = ring(3, x), ring(1, x)
 
-    def xg_copy(i, to, at):
-        return remote(gated.at[i, x], gated.at[i, x], xg_send.at[i, at], xg_recv.at[i, x], device(x_=to))
-
-    def xg_arrival(i, source, at):
-        return remote(gated.at[i, source], gated.at[i, source], xg_send.at[i, at], xg_recv.at[i, source], device(x_=source))
+    def half(i, source, at):
+        return gated.at[i, source, pl.ds(at * (ROWS // 2), ROWS // 2)]
+
+    def xg_copy(i, to, at, which):
+        ref = half(i, x, which)
+        return remote(ref, ref, xg_send.at[i, at, which], xg_recv.at[i, at, which], device(x_=to))
+
+    def xg_arrival(i, source, at, which):
+        ref = half(i, source, which)
+        return remote(ref, ref, xg_send.at[i, at, which], xg_recv.at[i, at, which], device(x_=source))
 
     def xr_copy(i, source, to, at):
-        ref = gated.at[i, source, pl.ds(at * (ROWS // 2), ROWS // 2)]
+        ref = half(i, source, at)
         return remote(ref, ref, xr_send.at[i, at], xr_recv.at[i, at], device(x_=to))
 
     def gate(i):
@@ -352,33 +354,36 @@
         for q in range(PEERS):
             query = short_filter(i * CHUNK + q * WIDTH)
             gated[i, x, :, q * WIDTH : (q + 1) * WIDTH] = (query * back[i, q].astype(F32)).astype(BF16)
-        xg_copy(i, right, 0).start()
-        xg_copy(i, left, 1).start()
+        xg_copy(i, right, 0, 0).start()
+        xg_copy(i, left, 1, 1).start()
+        xg_copy(i, right, 0, 1).start()
+        xg_copy(i, left, 1, 0).start()
 
     def relay(i):
-        xg_arrival(i, left, 0).wait_recv()
+        xg_arrival(i, left, 0, 0).wait_recv()
         xr_copy(i, left, right, 0).start()
-        xg_arrival(i, right, 1).wait_recv()
+        xg_arrival(i, right, 1, 1).wait_recv()
         xr_copy(i, right, left, 1).start()
 
     def far_arrivals(i):
         across = ring(2, x)
+        xg_arrival(i, left, 0, 1).wait_recv()
+        xg_arrival(i, right, 1, 0).wait_recv()
         xr_copy(i, across, left, 0).wait_recv()
         xr_copy(i, across, right, 1).wait_recv()
 
-    def project(group):
-        far_arrivals(2 * group)
-        far_arrivals(2 * group + 1)
+    def project(group, zh_):
         lhs = [gated[2 * group + part].reshape(PEERS * ROWS, CHUNK) for part in range(2)]
 
-        def block(j, carry):
+        def block(c, carry):
+            j = zh_ * 2 + c
             term = acc[j]
             for part in range(2):
                 term = term + dot(lhs[part], wts[j, pl.ds(pl.multiple_of(group * GROUP + part * CHUNK, CHUNK), CHUNK), :])
             acc[j] = term
             return carry
 
-        lax.fori_loop(0, PEERS, block, 0)
+        lax.fori_loop(0, 2, block, 0)
 
     def wy_copy(k):
         ref = quarter(wts.at[far_slot], ring(k, y))
@@ -411,12 +416,6 @@
 
         wc_copy(ring(k, y)).start()
 
-    def columns_last():
-        loads[7].wait()
-        mate_copy.wait_recv()
-        for which in range(PEERS):
-            wc_arrival(which).wait_recv()
-
     loads[5].wait()
     loads[6].wait()
     acc[...] = jnp.zeros(acc.shape, F32)
@@ -442,80 +441,107 @@
         def _():
             relay(t - 5)
 
+        @pl.when(t == 3)
+        def _():
+            mate_copy.start()
+
         @pl.when(t == 4)
         def _():
             columns_first()
 
         @pl.when(jnp.logical_or(t == 6, jnp.logical_or(t == 8, t == 10)))
         def _():
-            columns_next(t // 2 - 2)
-
-        @pl.when(t == 10)
-        def _():
-            columns_last()
-
-        @pl.when(t >= 10)
-        def _():
-            project(t - 10)
+            columns_next((t - 4) // 2)
+
+        @pl.when(t == 9)
+        def _():
+            loads[7].wait()
+            mate_copy.wait_recv()
+
+        @pl.when(t >= 9)
+        def _():
+            far_arrivals(2 * (t - 9))
+            far_arrivals(2 * (t - 9) + 1)
+            project(t - 9, zh)
 
         return carry
 
-    lax.fori_loop(0, CHUNKS + 5, step, 0)
-
-    mine = pl.ds(pl.multiple_of(x * OUT, OUT), OUT)
-
-    def out_copy(k):
+    lax.fori_loop(0, CHUNKS + 4, step, 0)
+
+    def out_columns(x_, zh_):
+        return out.at[:, pl.ds(pl.multiple_of(x_ * OUT + zh_ * (OUT // 2), OUT // 2), OUT // 2)]
+
+    def out_copy(zh_, k):
         q = ring(k, x)
-        return remote(outs.at[q], out.at[:, mine], o_send.at[k], o_recv.at[x], device(x_=q))
-
-    def out_arrival(k):
+        return remote(outs.at[zh_, q], out_columns(x, zh_), o_send.at[zh_, k], o_recv.at[zh_, x], device(x_=q))
+
+    def out_arrival(zh_, k):
         q = ring(k, x)
-        return remote(outs.at[q], out.at[:, pl.ds(pl.multiple_of(q * OUT, OUT), OUT)], o_send.at[k], o_recv.at[q], device(x_=q))
+        return remote(outs.at[zh_, q], out_columns(q, zh_), o_send.at[zh_, k], o_recv.at[zh_, q], device(x_=q))
+
+    def out_own(zh_):
+        return pltpu.make_async_copy(outs.at[zh_, x], out_columns(x, zh_), own_sem.at[zh_])
 
     last = GROUPS - 1
-    far_arrivals(2 * last)
-    far_arrivals(2 * last + 1)
-
-    def finish(k, carry):
-        q = ring(k, x)
-        lhs = jnp.concatenate([gated[2 * last, q], gated[2 * last + 1, q]], axis=1)
-        for j in range(PEERS):
-            total = acc[j, own_rows(q), :] + dot(lhs, wts[j, last * GROUP :, :])
-            outs[q, :, j * COLS : (j + 1) * COLS] = total.astype(BF16)
-
-        @pl.when(k < PEERS)
-        def _():
-            out_copy(k).start()
-
+
+    def finish(zh_):
+        def one(k, carry):
+            q = ring(k, x)
+            lhs = jnp.concatenate([gated[2 * last, q], gated[2 * last + 1, q]], axis=1)
+            for c in range(2):
+                j = zh_ * 2 + c
+                total = acc[j, own_rows(q), :] + dot(lhs, wts[j, last * GROUP :, :])
+                outs[zh_, q, :, c * COLS : (c + 1) * COLS] = total.astype(BF16)
+
+            @pl.when(k < PEERS)
+            def _():
+                out_copy(zh_, k).start()
+
+            return carry
+
+        lax.fori_loop(1, PEERS + 1, one, 0)
+        out_own(zh_).start()
+
+    relay(CHUNKS - 1)
+
+    def arrived(which, carry):
+        wc_arrival(which).wait_recv()
         return carry
 
-    lax.fori_loop(1, PEERS + 1, finish, 0)
-    own = pltpu.make_async_copy(outs.at[x], out.at[:, mine], local_sem.at[8])
-    own.start()
-    own.wait()
-    for k in range(1, PEERS):
-        out_arrival(k).wait_recv()
-
-    far_taps.wait_send()
+    lax.fori_loop(0, PEERS, arrived, 0)
+
+    def project_far(group, carry):
+        project(group, 1 - zh)
+        return carry
+
+    lax.fori_loop(0, last, project_far, 0)
+    for i in range(2 * last, CHUNKS):
+        far_arrivals(i)
+    finish(zh)
+    finish(1 - zh)
+    for zh_ in range(2):
+        out_own(zh_).wait()
+        for k in range(1, PEERS):
+            out_arrival(zh_, k).wait_recv()
+
     mate_copy.wait_send()
     for at in range(GROUPS + 2):
         halo_copy(at).wait_send()
 
-    def sent_taps(k, carry):
-        tap_copy(k, 0).wait_send()
-        tap_copy(k, 1).wait_send()
-        return carry
-
-    lax.fori_loop(1, NEAR, sent_taps, 0)
+    for k in range(1, NEAR):
+        tap_copy(k).wait_send()
 
     @pl.when(jnp.logical_or(zl == 0, zl == 3))
     def _():
         far_copy(0, 3 - zl).wait_send()
         far_copy(1, ring(2, zl)).wait_send()
+        far_taps(0, 3 - zl).wait_send()
+        far_taps(1, ring(2, zl)).wait_send()
 
     for k in range(1, PEERS):
         wy_copy(k - 1).wait_send()
-        out_copy(k).wait_send()
+        out_copy(0, k).wait_send()
+        out_copy(1, k).wait_send()
     for which in range(PEERS):
         wc_copy(which).wait_send()
 
@@ -523,8 +549,9 @@
         for k in range(1, PEERS):
             zf_copy(i, k).wait_send()
             zb_copy(i, k).wait_send()
-        xg_copy(i, right, 0).wait_send()
-        xg_copy(i, left, 1).wait_send()
+        for which in range(2):
+            xg_copy(i, right, 0, which).wait_send()
+            xg_copy(i, left, 1, which).wait_send()
         xr_copy(i, left, right, 0).wait_send()
         xr_copy(i, right, left, 1).wait_send()
 
@@ -545,15 +572,16 @@
         mixer_kernel,
         name="mixer",
         out_shape=jax.ShapeDtypeStruct((ROWS, CHANNELS), BF16),
-        in_specs=[anywhere, pl.BlockSpec(memory_space=pltpu.VMEM), pl.BlockSpec(memory_space=pltpu.VMEM)] + [anywhere] * 5,
+        in_specs=[anywhere, pl.BlockSpec(memory_space=pltpu.VMEM)] + [anywhere] * 6,
         out_specs=anywhere,
         scratch_shapes=[
             pltpu.VMEM((ROWS, 3 * CHANNELS), BF16),
             pltpu.VMEM((16, 3 * CHANNELS), BF16),
+            pltpu.VMEM((SPAN, FILTERS), BF16),
             pltpu.VMEM((GROUPS + 2, 2, 2 * HALO, HALF), BF16),
             pltpu.VMEM((GROUPS + 2, 2, 2 * HALO, HALF), BF16),
             pltpu.VMEM((HALO, 3 * CHANNELS), F32),
-            pltpu.VMEM((SHARDS, 16, TAPCOLS // 2), BF16),
+            pltpu.VMEM((NEAR, 2, 16, TAPCOLS // 2), BF16),
             pltpu.VMEM((8, 3 * CHANNELS), F32),
             pltpu.VMEM((2 * SPAN, SPAN), BF16),
             pltpu.VMEM((2 * SPAN, SPAN), BF16),
@@ -570,11 +598,11 @@
             pltpu.VMEM((CHUNKS, PEERS, ROWS, CHUNK), BF16),
             pltpu.VMEM((PEERS, CHANNELS, COLS), BF16),
             pltpu.VMEM((PEERS, PEERS * ROWS, COLS), F32),
-            pltpu.VMEM((PEERS, ROWS, OUT), BF16),
-            dma((10,)), dma((GROUPS + 2,)), dma((GROUPS + 2,)), dma((2, NEAR)), dma((SHARDS,)),
+            pltpu.VMEM((2, PEERS, ROWS, OUT // 2), BF16),
+            dma((11,)), dma((GROUPS + 2,)), dma((GROUPS + 2,)), dma((2,)), dma, dma((NEAR,)), dma((NEAR,)),
             dma((CHUNKS, PEERS)), dma((CHUNKS, PEERS)), dma((2, CHUNKS)), dma((CHUNKS, PEERS)), dma((CHUNKS, PEERS)),
-            dma((CHUNKS, 2)), dma((CHUNKS, PEERS)), dma((CHUNKS, 2)), dma((CHUNKS, 2)),
-            dma((2,)), dma, dma((PEERS,)), dma((PEERS,)), dma((2,)), dma((PEERS,)), dma((PEERS,)), dma((PEERS,)), dma((PEERS,)),
+            dma((CHUNKS, 2, 2)), dma((CHUNKS, 2, 2)), dma((CHUNKS, 2)), dma((CHUNKS, 2)),
+            dma((2,)), dma, dma((PEERS,)), dma((PEERS,)), dma((2,)), dma((PEERS,)), dma((PEERS,)), dma((2, PEERS)), dma((2, PEERS)), dma((2,)),
         ],
         compiler_params=pltpu.CompilerParams(collective_id=0, has_side_effects=True, vmem_limit_bytes=56 * 2**20),
     )(features[0], short_weight, long_filter, out_weight, *matrices)

time: 113 us -> 102 us (0.903)
  the two profiles are of different devices: /device:TPU:1 before, /device:TPU:16 now
where the time goes in v3:
time: 102 us
  Pallas kernels  99.3 us (97%)
  local copies, waits for them, and re-layouts  2.29 us (2%)
    pallas_call x1, Pallas kernels, shards(): pl.pallas_call(mixer_kernel, name='mixer', out_shape=jax.ShapeDtypeStruct...  99.3 us
    unnamed x1, local copies, waits for them, and re-layouts  2.29 us

profile of v3, /device:TPU:16, one launch (start us, length us, event | category | flops | bytes accessed | tf_op | source)
XLA Modules:
  0.0 101.6 jit_solution(5104283538656741677)
XLA Ops:
  0.0 99.3 %mixer.1 = bf16[128,4096]{1,0:T(8,128)(2,1)} custom-call(bf16[128,12288]{1,0:T(8,128)(2,1)} %bitcast.3, bf16[7,768]{1,0:T(8,128)(2,1)} %taps_in.1, bf16[512,256]{1,0:T(8,128)(2,1)} %filt_in.1, bf16[4096,256]{1,0:T(8,128)(2,1)} %weight.1, bf16[1024,512]{1,0:T(8,128)(2,1)} %constant.8.clone.fwd_hi_in, bf16[1024,512]{1,0:T(8,128)(2,1)} %constant.9.clone.fwd_lo_in, ...), custom_call_target="tpu_custom_call" | custom-call | tf_op jit(solution)/shard_map/mixer/pallas_call | solution.py:571
  99.4 2.3 %copy.10 = bf16[1,128,4096]{2,1,0:T(8,128)(2,1)} copy(bf16[1,128,4096]{2,1,0:T(8,128)(2,1)} %bitcast.2) | data formatting | bytes 2097152

commit v4 on v3

--- a/solution.py
+++ b/solution.py
@@ -232,12 +232,15 @@
     def own_rows(which):
         return pl.ds(pl.multiple_of(which * ROWS, ROWS), ROWS)
 
+    def across_first(k):
+        return (lax.rem(zl + 2, PEERS), 3 - zl, zl + 1 - 2 * lax.rem(zl, 2))[k - 1]
+
     def zf_copy(i, k):
-        q = ring(k, zl)
+        q = across_first(k)
         return remote(prod.at[i, q], cur.at[i, own_rows(zl)], zf_send.at[i, k], zf_recv.at[i, zl], device(zl_=q))
 
     def zf_arrival(i, k):
-        q = ring(k, zl)
+        q = across_first(k)
         return remote(prod.at[i, q], cur.at[i, own_rows(q)], zf_send.at[i, k], zf_recv.at[i, q], device(zl_=q))
 
     def products(i):
@@ -249,17 +252,16 @@
             unpack(group, 0, CHANNELS + group * GROUP)
             unpack(group, 1, 2 * CHANNELS + group * GROUP)
 
-        def one(q, inner):
+        def one(q):
             begin = i * CHUNK + q * WIDTH
             keys = short_filter(CHANNELS + begin)
             values = short_filter(2 * CHANNELS + begin)
-            prod[i, q] = (keys * values).astype(BF16)
-            return inner
-
-        lax.fori_loop(0, PEERS, one, 0)
+            return (keys * values).astype(BF16)
+
         for k in range(1, PEERS):
+            prod[i, across_first(k)] = one(across_first(k))
             zf_copy(i, k).start()
-        cur[i, own_rows(zl), :] = prod[i, zl]
+        cur[i, own_rows(zl), :] = one(zl)
 
         @pl.when(i == 1)
         def _():
@@ -279,11 +281,11 @@
             yf_copy(i).start()
 
     def zb_copy(i, k):
-        q = ring(k, zl)
+        q = across_first(k)
         return remote(convs.at[i, own_rows(q)], back.at[i, zl], zb_send.at[i, k], zb_recv.at[i, zl], device(zl_=q))
 
     def zb_arrival(i, k):
-        q = ring(k, zl)
+        q = across_first(k)
         return remote(convs.at[i, own_rows(q)], back.at[i, q], zb_send.at[i, k], zb_recv.at[i, q], device(zl_=q))
 
     def convolve(i):
@@ -312,17 +314,16 @@
 
         lax.fori_loop(0, 4, frequencies, 0)
 
-        def positions(part, carry):
+        def positions(part):
             rows = own_rows(part)
             both = dot(inv_hi[rows, :], jnp.concatenate([y_hi[...], y_lo[...]], axis=1))
             got = both[:, :WIDTH] + both[:, WIDTH:] + dot(inv_lo[rows, :], y_hi[...])
-            convs[i, rows, :] = got.astype(BF16)
-            return carry
-
-        lax.fori_loop(0, PEERS, positions, 0)
+            return got.astype(BF16)
+
         for k in range(1, PEERS):
+            convs[i, own_rows(across_first(k)), :] = positions(across_first(k))
             zb_copy(i, k).start()
-        back[i, zl] = convs[i, own_rows(zl), :]
+        back[i, zl] = positions(zl)
 
     left, right = ring(3, x), ring(1, x)
 

time: 102 us -> 101 us (level)
  no operation moved by 1% of the time
where the time goes in v4:
time: 101 us
  Pallas kernels  98.5 us (98%)
  local copies, waits for them, and re-layouts  2.29 us (2%)
    pallas_call x1, Pallas kernels, shards(): pl.pallas_call(mixer_kernel, name='mixer', out_shape=jax.ShapeDtypeStruct...  98.5 us
    unnamed x1, local copies, waits for them, and re-layouts  2.29 us

profile of v4, /device:TPU:16, one launch (start us, length us, event | category | flops | bytes accessed | tf_op | source)
XLA Modules:
  0.0 100.8 jit_solution(15978736158001992968)
XLA Ops:
  0.0 98.5 %mixer.1 = bf16[128,4096]{1,0:T(8,128)(2,1)} custom-call(bf16[128,12288]{1,0:T(8,128)(2,1)} %bitcast.3, bf16[7,768]{1,0:T(8,128)(2,1)} %taps_in.1, bf16[512,256]{1,0:T(8,128)(2,1)} %filt_in.1, bf16[4096,256]{1,0:T(8,128)(2,1)} %weight.1, bf16[1024,512]{1,0:T(8,128)(2,1)} %constant.8.clone.fwd_hi_in, bf16[1024,512]{1,0:T(8,128)(2,1)} %constant.9.clone.fwd_lo_in, ...), custom_call_target="tpu_custom_call" | custom-call | tf_op jit(solution)/shard_map/mixer/pallas_call | solution.py:572
  98.6 2.3 %copy.10 = bf16[1,128,4096]{2,1,0:T(8,128)(2,1)} copy(bf16[1,128,4096]{2,1,0:T(8,128)(2,1)} %bitcast.2) | data formatting | bytes 2097152

commit v5 on v4

--- a/solution.py
+++ b/solution.py
@@ -442,7 +442,7 @@
         def _():
             relay(t - 5)
 
-        @pl.when(t == 3)
+        @pl.when(t == 6)
         def _():
             mate_copy.start()
 
@@ -486,7 +486,7 @@
     last = GROUPS - 1
 
     def finish(zh_):
-        def one(k, carry):
+        def one(k):
             q = ring(k, x)
             lhs = jnp.concatenate([gated[2 * last, q], gated[2 * last + 1, q]], axis=1)
             for c in range(2):
@@ -494,13 +494,14 @@
                 total = acc[j, own_rows(q), :] + dot(lhs, wts[j, last * GROUP :, :])
                 outs[zh_, q, :, c * COLS : (c + 1) * COLS] = total.astype(BF16)
 
-            @pl.when(k < PEERS)
-            def _():
-                out_copy(zh_, k).start()
-
+        def send(step, carry):
+            k = lax.rem(step, PEERS - 1) + 1
+            one(k)
+            out_copy(zh_, k).start()
             return carry
 
-        lax.fori_loop(1, PEERS + 1, one, 0)
+        lax.fori_loop(1, PEERS, send, 0)
+        one(0)
         out_own(zh_).start()
 
     relay(CHUNKS - 1)

time: 101 us -> 100 us (0.990)
  Pallas kernels: 98.5 us -> 97.1 us
    pallas_call x1, Pallas kernels: 98.5 us -> 97.1 us  [shards(): pl.pallas_call(mixer_kernel, name='mixer', out_shape=jax.ShapeDtypeStruct...]
where the time goes in v5:
time: 100 us; the launch traced here: 99.4 us
  Pallas kernels  97.1 us (97%)
  local copies, waits for them, and re-layouts  2.29 us (2%)
    pallas_call x1, Pallas kernels, shards(): pl.pallas_call(mixer_kernel, name='mixer', out_shape=jax.ShapeDtypeStruct...  97.1 us
    unnamed x1, local copies, waits for them, and re-layouts  2.29 us

profile of v5, /device:TPU:16, one launch (start us, length us, event | category | flops | bytes accessed | tf_op | source)
XLA Modules:
  0.0 99.4 jit_solution(10417268619271886112)
XLA Ops:
  0.0 97.1 %mixer.1 = bf16[128,4096]{1,0:T(8,128)(2,1)} custom-call(bf16[128,12288]{1,0:T(8,128)(2,1)} %bitcast.3, bf16[7,768]{1,0:T(8,128)(2,1)} %taps_in.1, bf16[512,256]{1,0:T(8,128)(2,1)} %filt_in.1, bf16[4096,256]{1,0:T(8,128)(2,1)} %weight.1, bf16[1024,512]{1,0:T(8,128)(2,1)} %constant.8.clone.fwd_hi_in, bf16[1024,512]{1,0:T(8,128)(2,1)} %constant.9.clone.fwd_lo_in, ...), custom_call_target="tpu_custom_call" | custom-call | tf_op jit(solution)/shard_map/mixer/pallas_call | solution.py:573
  97.1 2.3 %copy.10 = bf16[1,128,4096]{2,1,0:T(8,128)(2,1)} copy(bf16[1,128,4096]{2,1,0:T(8,128)(2,1)} %bitcast.2) | data formatting | bytes 2097152
